TPU v7x, 512 devices: a whole 4x8x8 slice. The times are simulated.
512 devices in a mesh: gen: 32 (over z, y_lo), dat: 16 (over y_hi, x, core).
Axes of the slice: x: 4, y: 8 (y_hi: 2, y_lo: 4; y = y_hi * 4 + y_lo), z: 8, core: 2. Of those that a mesh axis runs over, the one named last changes fastest.
Arguments:
- gen_samples: bfloat16 [131072, 256], P(('gen', 'dat')), may hold values from -6 to 6
- data_samples: bfloat16 [12288, 256], P(('dat', 'gen')), may hold values from -6 to 6
- data_potential: float32 [12288], P(('dat', 'gen')), may hold values from -1 to 10
Outputs:
- gen_potential: float32 [131072], P(('gen', 'dat'))
- new_data_potential: float32 [12288], P(('dat', 'gen'))
All inputs are finite; a program needn't handle non-finite values.
Results may differ from a plain program's by a relative error of at most 0.0003.
Values may be sent and summed in bfloat16 or wider, within the bound.
A program may use at most 64 MiB of HBM per device.

v0:
```python
import jax
import jax.numpy as jnp
from jax import lax
from jax.sharding import PartitionSpec as P

EPS = 0.05


def combined_all(shard, axis, combine):
    everything = jax.tree.map(lambda part: lax.all_gather(part, axis), shard)
    initial = jax.tree.map(lambda part: part[0], everything)

    def turn(k, so_far):
        return combine(so_far, jax.tree.map(lambda part: part[k], everything))

    return lax.fori_loop(1, lax.axis_size(axis), turn, initial)


def pair_combine(first, second):
    top = jnp.maximum(first[0], second[0])
    return (top, first[1] * jnp.exp(first[0] - top) + second[1] * jnp.exp(second[0] - top))


def per_device(gen_samples, data_samples, data_potential):
    gen_rows = lax.all_gather(gen_samples, "dat", axis=0, tiled=True)
    data_rows = lax.all_gather(data_samples, "gen", axis=0, tiled=True)
    potential = lax.all_gather(data_potential, "gen", axis=0, tiled=True)
    width = gen_rows.shape[1]
    rows = gen_rows.shape[0]
    cols = data_rows.shape[0]
    n_dat = lax.axis_size("dat")
    n_gen = lax.axis_size("gen")
    sq_cols = jnp.sum(data_rows.astype(jnp.float32) ** 2, axis=1)
    block = min(512, rows)
    count = rows // block
    gen_blocks = gen_rows.reshape(count, block, width)

    def block_cost(tile_rows):
        sq_rows = jnp.sum(tile_rows.astype(jnp.float32) ** 2, axis=1)
        cross = lax.dot_general(
            tile_rows, data_rows, (((1,), (1,)), ((), ())), preferred_element_type=jnp.float32
        )
        return (sq_rows[:, None] + sq_cols[None, :] - 2.0 * cross) / width

    def row_pass(tile_rows):
        scores = (potential[None, :] - block_cost(tile_rows)) / EPS
        top = jnp.max(scores, axis=1)
        return (top, jnp.sum(jnp.exp(scores - top[:, None]), axis=1))

    row_max, row_sum = lax.map(row_pass, gen_blocks)
    row_max = row_max.reshape(rows)
    row_sum = row_sum.reshape(rows)
    log_cols = jnp.log(jnp.float32(cols * n_dat))
    share = rows // n_dat
    whole_max, whole_sum = combined_all((row_max, row_sum), "dat", pair_combine)
    gen_full = -EPS * (whole_max + jnp.log(whole_sum) - log_cols)
    gen_potential = lax.dynamic_slice_in_dim(gen_full, lax.axis_index("dat") * share, share, 0)

    def column_pass(carry, item):
        tile_rows, pot = item
        run_max, run_sum = carry
        scores = (pot[:, None] - block_cost(tile_rows)) / EPS
        top = jnp.maximum(run_max, jnp.max(scores, axis=0))
        run_sum = run_sum * jnp.exp(run_max - top) + jnp.sum(jnp.exp(scores - top[None, :]), axis=0)
        return ((top, run_sum), None)

    start = (jnp.full((cols,), -1e30, jnp.float32), jnp.zeros((cols,), jnp.float32))
    (col_max, col_sum), _ = lax.scan(
        column_pass, start, (gen_blocks, gen_full.reshape(count, block))
    )
    log_rows = jnp.log(jnp.float32(rows * n_gen))
    col_share = cols // n_gen
    all_max, all_sum = combined_all((col_max, col_sum), "gen", pair_combine)
    own_max = lax.dynamic_slice_in_dim(all_max, lax.axis_index("gen") * col_share, col_share, 0)
    own_sum = lax.dynamic_slice_in_dim(all_sum, lax.axis_index("gen") * col_share, col_share, 0)
    new_data_potential = -EPS * (own_max + jnp.log(own_sum) - log_rows)
    return (gen_potential, new_data_potential)


def solution(mesh):
    in_specs = (P(("gen", "dat"), None), P(("dat", "gen"), None), P(("dat", "gen")))
    out_specs = (P(("gen", "dat")), P(("dat", "gen")))
    return jax.shard_map(
        per_device, mesh=mesh, in_specs=in_specs, out_specs=out_specs, check_vma=False
    )
```

profile of v0, /device:TPU:10, one launch (start us, length us, event | category | flops | bytes accessed | tf_op | source)
XLA Modules:
  0.0 441.2 jit_solution(17504223152342963771)
XLA Ops:
  7.2 0.7 all-gather.8.cloned.1.call-update
  8.0 1.3 dynamic-slice
  9.9 0.9 dynamic-update-slice
  10.7 82.6 %all-reduce = f32[768]{0:T(1024)S(1)} all-reduce(f32[768]{0:T(1024)S(1)} %dynamic-update-slice), channel_id=1, replica_groups=mesh['gen'=32,'dat'=16] {'gen'}, use_global_device_ids=true, to_apply=%add | all-reduce | flops 768 | bytes 6144
  93.3 82.3 %all_gather.29 = bf16[768,256]{1,0:T(8,128)(2,1)S(1)} all-gather(bf16[24,256]{1,0:T(8,128)(2,1)} %param.12), channel_id=1, replica_groups=mesh['gen'=32,'dat'=16] {'gen'}, dimensions={0}, use_global_device_ids=true | all-gather | bytes 405504 | tf_op jit(solution)/shard_map/all_gather | solution.py:26
  175.6 0.2 multiply_reduce_fusion.2
  175.8 26.0 %while.59 = (s32[]{:T(128)}, f32[8,512]{1,0:T(8,128)S(1)}, f32[8,512]{1,0:T(8,128)S(1)}, f32[768]{0:T(1024)S(1)}, bf16[8,512,256]{2,1,0:T(8,128)(2,1)}, /*index=...) while((s32[]{:T(128)}, f32[8,512]{1,0:T(8,128)S(1)}, f32[8,512]{1,0:T(8,128)S(1)}, ...), condition=%wide.region_5.6_spmd, body=%wide.region_1.5_spmd.sunk | while | flops 205257216 | bytes 4088425 | solution.py:50
  175.9 1.1 multiply_reduce_fusion.5
  177.0 1.6 fusion.17
  178.6 0.4 exponential_reduce_fusion.4
  179.1 1.1 multiply_reduce_fusion.5
  180.2 1.6 fusion.17
  181.8 0.4 exponential_reduce_fusion.4
  182.4 1.1 multiply_reduce_fusion.5
  183.5 1.6 fusion.17
  185.1 0.4 exponential_reduce_fusion.4
  185.6 1.1 multiply_reduce_fusion.5
  186.7 1.6 fusion.17
  188.3 0.4 exponential_reduce_fusion.4
  188.9 1.1 multiply_reduce_fusion.5
  190.0 1.6 fusion.17
  191.6 0.4 exponential_reduce_fusion.4
  192.1 1.1 multiply_reduce_fusion.5
  193.2 1.6 fusion.17
  194.8 0.4 exponential_reduce_fusion.4
  195.4 1.1 multiply_reduce_fusion.5
  196.5 1.6 fusion.17
  198.1 0.4 exponential_reduce_fusion.4
  198.6 1.1 multiply_reduce_fusion.5
  199.7 1.6 fusion.17
  201.3 0.4 exponential_reduce_fusion.4
  201.9 25.0 %all-gather.2 = f32[16,1,4096]{2,1,0:T(1,128)S(1)} all-gather(f32[1,1,4096]{2,1,0:T(1,128)S(1)} %reshape.30), channel_id=1, replica_groups=mesh['gen'=32,'dat'=16] {'dat'}, dimensions={0}, use_global_device_ids=true | all-gather | bytes 278528 | tf_op jit(solution)/shard_map/all_gather | solution.py:10
  227.0 29.1 %all-gather.3 = f32[16,1,4096]{2,1,0:T(1,128)S(1)} all-gather(f32[1,1,4096]{2,1,0:T(1,128)S(1)} %reshape.32), channel_id=1, replica_groups=mesh['gen'=32,'dat'=16] {'dat'}, dimensions={0}, use_global_device_ids=true | all-gather | bytes 278528 | tf_op jit(solution)/shard_map/all_gather | solution.py:10
  256.3 1.3 while.60
  257.6 23.7 %while.62 = (s32[]{:T(128)}, f32[768]{0:T(1024)S(1)}, f32[768]{0:T(1024)S(1)}, f32[8,512]{1,0:T(8,128)S(1)}, bf16[8,512,256]{2,1,0:T(8,128)(2,1)}, /*index=5*/f3...) while((s32[]{:T(128)}, f32[768]{0:T(1024)S(1)}, f32[768]{0:T(1024)S(1)}, ...), condition=%wide.region_12.13_spmd.clone, body=%wide.region_8.12_spmd.clone.sunk | while | flops 205262080 | bytes 4117104 | solution.py:68
  257.6 1.1 multiply_reduce_fusion.6
  258.7 1.5 fusion.19
  260.3 0.3 exponential_reduce_fusion.5
  260.5 1.1 multiply_reduce_fusion.6
  261.7 1.5 fusion.19
  263.2 0.3 exponential_reduce_fusion.5
  263.5 1.1 multiply_reduce_fusion.6
  264.6 1.5 fusion.19
  266.2 0.3 exponential_reduce_fusion.5
  266.5 1.1 multiply_reduce_fusion.6
  267.6 1.5 fusion.19
  269.1 0.3 exponential_reduce_fusion.5
  269.4 1.1 multiply_reduce_fusion.6
  270.5 1.5 fusion.19
  272.1 0.3 exponential_reduce_fusion.5
  272.4 1.1 multiply_reduce_fusion.6
  273.5 1.5 fusion.19
  275.0 0.3 exponential_reduce_fusion.5
  275.3 1.1 multiply_reduce_fusion.6
  276.5 1.5 fusion.19
  278.0 0.3 exponential_reduce_fusion.5
  278.3 1.1 multiply_reduce_fusion.6
  279.4 1.5 fusion.19
  281.0 0.3 exponential_reduce_fusion.5
  281.3 74.0 %all-gather.5 = f32[32,1,768]{2,1,0:T(1,128)S(1)} all-gather(f32[1,1,768]{2,1,0:T(1,128)S(1)} %reshape.36), channel_id=3, replica_groups=mesh['gen'=32,'dat'=16] {'gen'}, dimensions={0}, use_global_device_ids=true | all-gather | bytes 101376 | tf_op jit(solution)/shard_map/all_gather | solution.py:10
  355.3 75.5 %all-gather.4 = f32[32,1,768]{2,1,0:T(1,128)S(1)} all-gather(f32[1,1,768]{2,1,0:T(1,128)S(1)} %reshape.34), channel_id=2, replica_groups=mesh['gen'=32,'dat'=16] {'gen'}, dimensions={0}, use_global_device_ids=true | all-gather | bytes 101376 | tf_op jit(solution)/shard_map/all_gather | solution.py:10
  430.8 2.3 while.61
  433.1 0.6 dynamic_slice.60
  433.8 0.6 add_multiply_fusion.1
  (161 shorter events, 3.8 us)
Async XLA Ops:
  7.2 168.7 %all-gather.8.cloned.1.call-start = ((), (), s32[]{:S(2)}) async-start(), calls=%async_computation | async-start | bytes 2228224 | tf_op jit(solution)/shard_map/all_gather | solution.py:25
Sparse Core Ops, SparseCore 0:
  11.3 71.9 all-gather.7
where the time goes:
time: 442 us; the launch traced here: 441 us
  blocking collectives  368 us (83%)
  matrix products  25 us (6%)
  other arithmetic  24.5 us (6%)
  between operations  14.8 us (3%)
  local copies, waits for them, and re-layouts  5.65 us (1%)
    all_gather x4, blocking collectives, combined_all(): everything = jax.tree.map(lambda part: lax.all_gather(part, axis), shard)  204 us
    unnamed x1, blocking collectives  82.6 us
    all_gather x1, blocking collectives, per_device(): data_rows = lax.all_gather(data_samples, 'gen', axis=0, tiled=True)  82.3 us
    dot_general x16, matrix products, block_cost(): lax.dot_general(tile_rows, data_rows, (((1,), (1,)), ((), ())), preferred...  25 us
    reduce_sum x16, other arithmetic, block_cost(): sq_rows = jnp.sum(tile_rows.astype(jnp.float32) ** 2, axis=1)  17.6 us
  transfers between devices with their start and end apart: 1, of which 0 were waited for; matrix products, arithmetic and copies ran while one was open for 1% of the time, Pallas kernels for 0%

commit v1 on v0

v1 whole, which is shorter than its diff:
```python
import math

import jax
import jax.numpy as jnp
from jax import lax
from jax.experimental import pallas as pl
from jax.experimental.pallas import tpu as pltpu
from jax.sharding import PartitionSpec as P

EPS = 0.05
LOG2E = math.log2(math.e)
LN2 = math.log(2.0)
SCALE = LOG2E / EPS
LOW = -1e30
MESH = pl.DeviceIdType.MESH
F32 = jnp.float32
BF16 = jnp.bfloat16

NX, NY, NZ, NC = 4, 8, 8, 2
CHIPS = NY * NZ
ROWS = 256
COLS = 24
WIDTH = 256
HALF = WIDTH // 2
UNIT = 8
UCOLS = UNIT * COLS
KEEP = 1.0 / WIDTH


def hops(d):
    return min(d % 8, -d % 8)


LATTICE = sorted(
    [(p, q) for q in range(8) for p in range(8) if (p + 2 * q) % 4 == 0 and (p, q) != (0, 0)],
    key=lambda o: -(hops(o[0]) + hops(o[1])),
)


def squares(values):
    wide = values.astype(F32)
    wide = wide * wide
    high = wide.astype(BF16)
    low = (wide - high.astype(F32)).astype(BF16)
    ones = jnp.ones((8, WIDTH), BF16)
    dims = (((1,), (1,)), ((), ()))
    return lax.dot_general(ones, high, dims, preferred_element_type=F32) + lax.dot_general(
        ones, low, dims, preferred_element_type=F32
    )


def kernel(
    gen_hbm, data_ref, pot_ref, f_out, g_out,
    x_buf, own, sib, own_u, sib_u, stash, row_m, row_s, row_l, send_l, send_c, recv_c, final,
    local_sem, x_send, x_recv, one_send, one_recv, two_send, two_recv, sib_send, sib_recv,
    row_send, row_recv, col_send, col_recv, fin_send, fin_recv,
):
    gen = lax.axis_index("gen")
    dat = lax.axis_index("dat")
    x, c = (dat // 2) % NX, dat % 2
    y, z = (dat // 8) * 4 + gen % 4, gen // 4

    def device(x_, y_, z_, c_):
        return (z_ * 4 + y_ % 4, (y_ // 4) * 8 + x_ * 2 + c_)

    p, q = y + c * (z - y), z + c * (y - z)

    def in_plane(p_, q_):
        p_, q_ = p_ % 8, q_ % 8
        return device(x, p_ + c * (q_ - p_), q_ + c * (p_ - q_), c)

    def slot_of(p_, q_):
        return ((p_ + 2 * q_) % 4) * 16 + q_ * 2 + p_ // 4

    sibling = device(x, y, z, 1 - c)
    x_peers = [device((x + d) % NX, y, z, c) for d in (2, 1, 3)]
    near = [in_plane(p + 1, q), in_plane(p - 1, q), in_plane(p, q + 1), in_plane(p, q - 1)]
    group = [in_plane(p + dp, q + dq) for dp, dq in LATTICE]
    peers = group + near + x_peers + [sibling]

    barrier = pltpu.get_barrier_semaphore()
    for peer in peers:
        pl.semaphore_signal(barrier, inc=1, device_id=peer, device_id_type=MESH)

    load = pltpu.make_async_copy(gen_hbm, x_buf.at[x], local_sem)
    load.start()

    mine = slot_of(p, q)
    data = data_ref[...].astype(F32)
    own[mine] = jnp.concatenate([data[:, :HALF], data[:, HALF:]], axis=0).astype(BF16)
    term = (pot_ref[...] - squares(data_ref[...])[0:1, :] * KEEP) * SCALE
    own_u[mine] = jnp.concatenate([term, jnp.zeros((1, 128 - COLS), F32)], axis=1)
    row_m[...] = jnp.full(row_m.shape, LOW, F32)
    row_s[...] = jnp.zeros(row_s.shape, F32)

    pl.semaphore_wait(barrier, len(peers))

    def remote(src, dst, send, recv, peer):
        return pltpu.make_async_remote_copy(
            src_ref=src, dst_ref=dst, send_sem=send, recv_sem=recv, device_id=peer, device_id_type=MESH
        )

    for peer in group:
        remote(own.at[mine], own.at[mine], one_send.at[0], one_recv.at[0], peer).start()
        remote(own_u.at[mine], own_u.at[mine], one_send.at[1], one_recv.at[1], peer).start()
    for peer in x_peers:
        remote(gen_hbm, x_buf.at[x], x_send, x_recv, peer).start()

    one = [
        remote(own.at[pl.ds(0, 15)], own.at[pl.ds(0, 15)], one_send.at[0], one_recv.at[0], sibling),
        remote(own_u.at[pl.ds(0, 15)], own_u.at[pl.ds(0, 15)], one_send.at[1], one_recv.at[1], sibling),
    ]
    for copy in one:
        copy.wait_recv()

    kind = (p + 2 * q) % 4
    base = kind * 16

    def block(ref, start):
        return ref.at[pl.ds(start, UNIT)]

    def to_near(k, start, peer):
        return [
            remote(block(own, start), block(own, start), two_send.at[0, k], two_recv.at[0, k], peer),
            remote(block(own_u, start), block(own_u, start), two_send.at[1, k], two_recv.at[1, k], peer),
        ]

    def to_sibling(k, start):
        return [
            remote(block(own, start), block(sib, start), sib_send.at[0, k], sib_recv.at[0, k], sibling),
            remote(block(own_u, start), block(sib_u, start), sib_send.at[1, k], sib_recv.at[1, k], sibling),
        ]

    outgoing = (
        to_near(0, base, near[0]) + to_near(1, base, near[1])
        + to_near(2, base + 8, near[0]) + to_near(3, base + 8, near[1])
        + to_near(4, base, near[2]) + to_near(5, base + 8, near[3])
    )
    for copy in outgoing:
        copy.start()
    for k in range(2):
        for copy in to_sibling(k, base + 8 * k):
            copy.start()

    load.wait()
    gather_x = remote(x_buf.at[pl.ds(0, 3)], x_buf.at[pl.ds(0, 3)], x_send, x_recv, sibling)
    gather_x.wait_recv()

    lane = lax.broadcasted_iota(jnp.int32, (UNIT, COLS, 128), 2)
    sub = lax.broadcasted_iota(jnp.int32, (UNIT, COLS, 128), 1)
    on_diagonal = lane == sub

    def row_unit(data_blocks, terms, place):
        wide = data_blocks[...].astype(F32)
        first = wide[:, :COLS, :].reshape(UCOLS, HALF)
        second = wide[:, COLS:, :].reshape(UCOLS, HALF)
        cols = jnp.concatenate([first.astype(BF16), second.astype(BF16)], axis=1)
        spread = jnp.where(on_diagonal, jnp.broadcast_to(terms[...], (UNIT, COLS, 128)), 0.0)
        term_ = jnp.sum(spread, axis=2, keepdims=True).reshape(UCOLS, 1)
        for b in range(NX):
            lanes = slice(b * ROWS, (b + 1) * ROWS)
            cross = lax.dot_general(cols, x_buf[b], (((1,), (1,)), ((), ())), preferred_element_type=F32)
            scores = cross * (2.0 * KEEP * SCALE) + term_
            stash[pl.ds(place, UNIT), :, lanes] = scores.reshape(UNIT, COLS, ROWS)
            parts = scores.reshape(UCOLS // 8, 8, ROWS)
            old = row_m[:, lanes]
            top = jnp.maximum(old, jnp.max(parts, axis=0))
            row_m[:, lanes] = top
            row_s[:, lanes] = row_s[:, lanes] * jnp.exp2(old - top) + jnp.sum(
                jnp.exp2(parts - top[None]), axis=0
            )

    def own_unit(start):
        row_unit(block(own, start), block(own_u, start), start)

    def sib_unit(start):
        row_unit(block(sib, start), block(sib_u, start), CHIPS + start)

    sp, sq = q, p
    sib_kind = (sp + 2 * sq) % 4

    def arrival(k, kind_):
        far = k // 4
        which = (kind_ + (1 - far) * (2 * (k % 2) - 1) + 2 * far) % 4
        half = (1 - far) * (k // 2) + far * (k % 4)
        return which * 16 + half * 8

    def first_units(k, _):
        own_unit(base + 8 * k)
        return 0

    lax.fori_loop(0, 2, first_units, 0)

    def first_sib(k, _):
        for copy in to_sibling(k, sib_kind * 16 + 8 * k):
            copy.wait_recv()
        sib_unit(sib_kind * 16 + 8 * k)
        return 0

    lax.fori_loop(0, 2, first_sib, 0)

    def next_units(k, _):
        start = arrival(k, kind)
        for copy in to_near(k, start, near[0]):
            copy.wait_recv()
        for copy in to_sibling(k + 2, start):
            copy.start()
        own_unit(start)
        return 0

    lax.fori_loop(0, 6, next_units, 0)

    def next_sib(k, _):
        start = arrival(k, sib_kind)
        for copy in to_sibling(k + 2, start):
            copy.wait_recv()
        sib_unit(start)
        return 0

    lax.fori_loop(0, 6, next_sib, 0)

    m = row_m[...]
    top = jnp.max(m, axis=0, keepdims=True)
    total = jnp.sum(row_s[...] * jnp.exp2(m - top), axis=0, keepdims=True)
    row_l[x] = top + jnp.log2(total)
    for peer in x_peers:
        remote(row_l.at[x], row_l.at[x], row_send, row_recv, peer).start()
    gather_l = remote(row_l.at[pl.ds(0, 3)], row_l.at[pl.ds(0, 3)], row_send, row_recv, sibling)
    gather_l.wait_recv()
    parts = [row_l[b] for b in range(NX)]
    top = jnp.maximum(jnp.maximum(parts[0], parts[1]), jnp.maximum(parts[2], parts[3]))
    total = sum(jnp.exp2(part - top) for part in parts)
    whole = top + jnp.log2(total)
    for b in range(NX):
        send_l[b] = whole[:, b * ROWS : (b + 1) * ROWS]
    lifted = jnp.broadcast_to(whole, (8, NX * ROWS))

    lane2 = lax.broadcasted_iota(jnp.int32, (COLS, 128), 1)
    sub2 = lax.broadcasted_iota(jnp.int32, (COLS, 128), 0)
    at_own = lane2 == sub2
    at_sib = lane2 == sub2 + 64

    def col_scores(place):
        scores = stash[place].reshape(COLS // 8, 8, NX * ROWS) - lifted[None]
        pieces = [scores[:, :, i * 128 : (i + 1) * 128] for i in range(NX * ROWS // 128)]
        peak = pieces[0]
        for piece in pieces[1:]:
            peak = jnp.maximum(peak, piece)
        added = jnp.exp2(pieces[0] - peak)
        for piece in pieces[1:]:
            added = added + jnp.exp2(piece - peak)
        peak, added = peak.reshape(COLS, 128), added.reshape(COLS, 128)
        crest = jnp.max(peak, axis=1, keepdims=True)
        return crest + jnp.log2(jnp.sum(added * jnp.exp2(peak - crest), axis=1, keepdims=True))

    here = y * 8 + z

    def far_first(i):
        return (4 + (i % 2) * ((i + 1) // 2) - (1 - i % 2) * (i // 2)) % 8

    def columns(i, _):
        y_ = (y + far_first(i)) % 8
        for j in range(8):
            z_ = (z + far_first(j)) % 8
            p_, q_ = y_ + c * (z_ - y_), z_ + c * (y_ - z_)
            first = col_scores(slot_of(p_, q_))
            second = col_scores(CHIPS + slot_of(q_, p_))
            line = jnp.where(at_own, first, 0.0) + jnp.where(at_sib, second, 0.0)
            line = jnp.sum(line, axis=0, keepdims=True)
            there = y_ * 8 + z_
            if j < 7:
                send_c[there] = line
                remote(send_c.at[there], recv_c.at[here], col_send, col_recv, device(x, y_, z_, c)).start()
            else:

                @pl.when(i < 7)
                def _(line=line, there=there, y_=y_, z_=z_):
                    send_c[there] = line
                    remote(send_c.at[there], recv_c.at[here], col_send, col_recv, device(x, y_, z_, c)).start()

                @pl.when(i == 7)
                def _(line=line):
                    recv_c[here] = line

        return 0

    lax.fori_loop(0, 8, columns, 0)

    sq_rows = squares(x_buf[x])[0:1, :]
    f_out[...] = sq_rows * KEEP - (EPS * LN2) * send_l[x] + EPS * math.log(float(CHIPS * NX * NC * COLS))

    gather_c = remote(recv_c.at[pl.ds(0, CHIPS - 1)], recv_c.at[pl.ds(0, CHIPS - 1)], col_send, col_recv, sibling)
    gather_c.wait_recv()
    lines = recv_c[...]
    top = jnp.max(lines, axis=0)
    final[0] = top + jnp.log2(jnp.sum(jnp.exp2(lines - top[None]), axis=0))
    swap = remote(final.at[0], final.at[1], fin_send, fin_recv, sibling)
    swap.start()
    swap.wait_recv()
    ours, theirs = final[0][:, :COLS], final[1][:, 64 : 64 + COLS]
    top = jnp.maximum(ours, theirs)
    score = top + jnp.log2(jnp.exp2(ours - top) + jnp.exp2(theirs - top))
    g_out[...] = pot_ref[...] - (EPS * LN2) * score + EPS * (
        math.log(float(CHIPS * NX * NC * ROWS)) - math.log(float(CHIPS * NX * NC * COLS))
    )

    for copy in one + [gather_x, gather_l, gather_c, swap] + outgoing:
        copy.wait_send()

    def sent(k, _):
        for copy in to_sibling(k, 0):
            copy.wait_send()
        return 0

    lax.fori_loop(0, 8, sent, 0)


def per_device(gen_samples, data_samples, data_potential):
    vmem = pl.BlockSpec(memory_space=pltpu.VMEM)
    dma = pltpu.SemaphoreType.DMA
    f, g = pl.pallas_call(
        kernel,
        out_shape=(jax.ShapeDtypeStruct((1, ROWS), F32), jax.ShapeDtypeStruct((1, COLS), F32)),
        in_specs=[pl.BlockSpec(memory_space=pl.ANY), vmem, vmem],
        out_specs=(vmem, vmem),
        scratch_shapes=[
            pltpu.VMEM((NX, ROWS, WIDTH), BF16),
            pltpu.VMEM((CHIPS, 2 * COLS, HALF), BF16),
            pltpu.VMEM((CHIPS, 2 * COLS, HALF), BF16),
            pltpu.VMEM((CHIPS, 1, 128), F32),
            pltpu.VMEM((CHIPS, 1, 128), F32),
            pltpu.VMEM((2 * CHIPS, COLS, NX * ROWS), F32),
            pltpu.VMEM((8, NX * ROWS), F32),
            pltpu.VMEM((8, NX * ROWS), F32),
            pltpu.VMEM((NX, 1, NX * ROWS), F32),
            pltpu.VMEM((NX, 1, ROWS), F32),
            pltpu.VMEM((CHIPS, 1, 128), F32),
            pltpu.VMEM((CHIPS, 1, 128), F32),
            pltpu.VMEM((2, 1, 128), F32),
            dma, dma, dma,
            dma((2,)), dma((2,)), dma((2, 6)), dma((2, 6)), dma((2, 8)), dma((2, 8)),
            dma, dma, dma, dma, dma, dma,
        ],
        compiler_params=pltpu.CompilerParams(
            collective_id=0, has_side_effects=True, vmem_limit_bytes=40 * 2**20
        ),
    )(gen_samples, data_samples, data_potential.reshape(1, COLS))
    return f.reshape(ROWS), g.reshape(COLS)


def solution(mesh):
    in_specs = (P(("gen", "dat"), None), P(("dat", "gen"), None), P(("dat", "gen")))
    out_specs = (P(("gen", "dat")), P(("dat", "gen")))
    return jax.shard_map(
        per_device, mesh=mesh, in_specs=in_specs, out_specs=out_specs, check_vma=False
    )
```

time: 442 us -> 62 us (0.14)
  the two profiles are of different devices: /device:TPU:10 before, /device:TPU:1 now
where the time goes in v1:
time: 62 us; the launch traced here: 61.8 us
  Pallas kernels  57.8 us (93%)
  local copies, waits for them, and re-layouts  3.33 us (5%)
  between operations  0.65 us (1%)
    pallas_call x1, Pallas kernels, per_device(): pl.pallas_call(kernel, out_shape=(jax.ShapeDtypeStruct((1, ROWS), F32), j...  57.8 us
    unnamed x8, local copies, waits for them, and re-layouts  3.33 us

profile of v1, /device:TPU:1, one launch (start us, length us, event | category | flops | bytes accessed | tf_op | source)
XLA Modules:
  0.0 61.8 jit_solution(10441083477859067604)
XLA Ops:
  0.6 0.0 copy-start.2
  0.6 0.6 %copy-done.2 = f32[24]{0:T(128)S(1)} copy-done((f32[24]{0:T(128)S(1)}, f32[24]{0:T(128)}, u32[]{:S(2)}) %copy-start.2) | copy-done | bytes 120
  1.3 0.0 copy-start
  1.3 0.9 %copy-done = bf16[256,256]{1,0:T(8,128)(2,1)S(1)} copy-done((bf16[256,256]{1,0:T(8,128)(2,1)S(1)}, bf16[256,256]{1,0:T(8,128)(2,1)}, u32[]{:S(2)}) %copy-start) | copy-done | bytes 131096
  2.2 0.0 copy-start.1
  2.2 0.7 %copy-done.1 = bf16[24,256]{1,0:T(8,128)(2,1)S(1)} copy-done((bf16[24,256]{1,0:T(8,128)(2,1)S(1)}, bf16[24,256]{1,0:T(8,128)(2,1)}, u32[]{:S(2)}) %copy-start.1) | copy-done | bytes 12312
  2.9 57.8 %shard_map.50 = (f32[1,256]{1,0:T(1,128)S(1)}, f32[1,24]{1,0:T(1,128)S(1)}) custom-call(bf16[256,256]{1,0:T(8,128)(2,1)S(1)} %copy-done, bf16[24,256]{1,0:T(8,128)(2,1)S(1)} %copy-done.1, f32[1,24]{1,0:T(1,128)S(1)} %bitcast.4), custom_call_target="tpu_custom_call" | custom-call | tf_op jit(solution)/shard_map/pallas_call | solution.py:321
  60.8 0.6 copy.7
  61.3 0.5 copy.8
Async XLA Ops:
  0.6 0.7 %copy-start.2 = (f32[24]{0:T(128)S(1)}, f32[24]{0:T(128)}, u32[]{:S(2)}) copy-start(f32[24]{0:T(128)} %param.5) | copy-start | bytes 292
  1.3 0.9 %copy-start = (bf16[256,256]{1,0:T(8,128)(2,1)S(1)}, bf16[256,256]{1,0:T(8,128)(2,1)}, u32[]{:S(2)}) copy-start(bf16[256,256]{1,0:T(8,128)(2,1)} %gen_hbm.1) | copy-start | bytes 393220
  2.2 0.7 %copy-start.1 = (bf16[24,256]{1,0:T(8,128)(2,1)S(1)}, bf16[24,256]{1,0:T(8,128)(2,1)}, u32[]{:S(2)}) copy-start(bf16[24,256]{1,0:T(8,128)(2,1)} %data_ref.1) | copy-start | bytes 36868

commit v2 on v1

v2 whole, which is shorter than its diff:
```python
import math

import jax
import jax.numpy as jnp
from jax import lax
from jax.experimental import pallas as pl
from jax.experimental.pallas import tpu as pltpu
from jax.sharding import PartitionSpec as P

EPS = 0.05
LOG2E = math.log2(math.e)
LN2 = math.log(2.0)
SCALE = LOG2E / EPS
LOW = -1e30
MESH = pl.DeviceIdType.MESH
F32 = jnp.float32
BF16 = jnp.bfloat16

NX, NY, NZ, NC = 4, 8, 8, 2
CHIPS = NY * NZ
ROWS = 256
COLS = 24
WIDTH = 256
HALF = WIDTH // 2
UNIT = 16
UCOLS = UNIT * COLS
KEEP = 1.0 / WIDTH


def hops(d):
    return min(d % 8, -d % 8)


LATTICE = sorted(
    [(p, q) for q in range(8) for p in range(8) if (p + 2 * q) % 4 == 0 and (p, q) != (0, 0)],
    key=lambda o: -(hops(o[0]) + hops(o[1])),
)


def squares(values):
    wide = values.astype(F32)
    wide = wide * wide
    high = wide.astype(BF16)
    low = (wide - high.astype(F32)).astype(BF16)
    ones = jnp.ones((8, WIDTH), BF16)
    dims = (((1,), (1,)), ((), ()))
    return lax.dot_general(ones, high, dims, preferred_element_type=F32) + lax.dot_general(
        ones, low, dims, preferred_element_type=F32
    )


def kernel(
    gen_hbm, data_hbm, pot_hbm, f_out, g_out,
    x_buf, data_buf, pot_buf, sq_buf, blocks, terms, stash, row_m, row_s, row_l, send_l,
    peak_a, added_a, peak_b, added_b, send_q, recv_q, send_p, recv_p, final,
    local_sem, x_send, x_recv, one_send, one_recv, two_send, two_recv, sib_send, sib_recv,
    row_send, row_recv, q_send, q_recv, p_send, p_recv, fin_send, fin_recv,
):
    gen = lax.axis_index("gen")
    dat = lax.axis_index("dat")
    x, c = (dat // 2) % NX, dat % 2
    y, z = (dat // 8) * 4 + gen % 4, gen // 4

    def device(x_, y_, z_, c_):
        return (z_ * 4 + y_ % 4, (y_ // 4) * 8 + x_ * 2 + c_)

    p, q = y + c * (z - y), z + c * (y - z)

    def in_plane(p_, q_):
        p_, q_ = p_ % 8, q_ % 8
        return device(x, p_ + c * (q_ - p_), q_ + c * (p_ - q_), c)

    def slot_of(p_, q_):
        return ((p_ + 2 * q_) % 4) * 16 + q_ * 2 + p_ // 4

    sibling = device(x, y, z, 1 - c)
    x_peers = [device((x + d) % NX, y, z, c) for d in (2, 1, 3)]
    near = [in_plane(p + 1, q), in_plane(p - 1, q), in_plane(p, q + 1), in_plane(p, q - 1)]
    group = [in_plane(p + dp, q + dq) for dp, dq in LATTICE]

    loads = [
        pltpu.make_async_copy(data_hbm, data_buf, local_sem.at[0]),
        pltpu.make_async_copy(pot_hbm, pot_buf, local_sem.at[1]),
        pltpu.make_async_copy(gen_hbm, x_buf.at[x], local_sem.at[2]),
    ]
    for copy in loads:
        copy.start()

    peers = group + near + x_peers + [sibling]
    barrier = pltpu.get_barrier_semaphore()
    for peer in peers:
        pl.semaphore_signal(barrier, inc=1, device_id=peer, device_id_type=MESH)

    mine = slot_of(p, q)
    for copy in loads[:2]:
        copy.wait()
    data = data_buf[...].astype(F32)
    blocks[mine] = jnp.concatenate([data[:, :HALF], data[:, HALF:]], axis=0).astype(BF16)
    term = (pot_buf[...] - squares(data_buf[...])[0:1, :] * KEEP) * SCALE
    terms[mine] = jnp.concatenate([term, jnp.zeros((1, 128 - COLS), F32)], axis=1)

    pl.semaphore_wait(barrier, len(peers))

    def remote(src, dst, send, recv, peer):
        return pltpu.make_async_remote_copy(
            src_ref=src, dst_ref=dst, send_sem=send, recv_sem=recv, device_id=peer, device_id_type=MESH
        )

    for peer in group:
        remote(blocks.at[mine], blocks.at[mine], one_send.at[0], one_recv.at[0], peer).start()
    for peer in x_peers:
        remote(gen_hbm, x_buf.at[x], x_send, x_recv, peer).start()
    for peer in group:
        remote(terms.at[mine], terms.at[mine], one_send.at[1], one_recv.at[1], peer).start()

    row_m[...] = jnp.full(row_m.shape, LOW, F32)
    row_s[...] = jnp.zeros(row_s.shape, F32)
    loads[2].wait()
    sq_buf[...] = squares(x_buf[x])[0:1, :]

    one = [
        remote(ref.at[pl.ds(0, 15)], ref.at[pl.ds(0, 15)], one_send.at[i], one_recv.at[i], sibling)
        for i, ref in enumerate((blocks, terms))
    ]
    for copy in one:
        copy.wait_recv()

    kind, sib_kind = (p + 2 * q) % 4, (q + 2 * p) % 4

    def to_near(k, start, count, peer):
        return [
            remote(ref.at[pl.ds(start, count)], ref.at[pl.ds(start, count)], two_send.at[i, k], two_recv.at[i, k], peer)
            for i, ref in enumerate((blocks, terms))
        ]

    def to_sibling(k, start):
        return [
            remote(ref.at[pl.ds(start, 16)], ref.at[pl.ds(CHIPS + start, 16)], sib_send.at[i, k], sib_recv.at[i, k], sibling)
            for i, ref in enumerate((blocks, terms))
        ]

    base = kind * 16
    outgoing = (
        to_near(2, base, 8, near[2]) + to_near(3, base + 8, 8, near[3])
        + to_near(0, base, 16, near[0]) + to_near(1, base, 16, near[1])
    )
    for copy in outgoing:
        copy.start()
    for copy in to_sibling(0, base):
        copy.start()

    gather_x = remote(x_buf.at[pl.ds(0, 3)], x_buf.at[pl.ds(0, 3)], x_send, x_recv, sibling)
    gather_x.wait_recv()

    def place(k, kind_):
        return ((kind_ + 2 * k + 3 * (k // 2)) % 4) * 16

    lane = lax.broadcasted_iota(jnp.int32, (UNIT, COLS, 128), 2)
    sub = lax.broadcasted_iota(jnp.int32, (UNIT, COLS, 128), 1)
    on_diagonal = lane == sub

    def row_unit(step, _):
        k, other = step // 2, step % 2
        mine_at, sib_at = place(k, kind), place(k, sib_kind)

        @pl.when(step == 2)
        def _():
            for copy in to_near(2, base, 8, near[2]) + to_near(3, base, 8, near[3]):
                copy.wait_recv()

        @pl.when((step >= 4) & (other == 0))
        def _():
            for copy in to_near(k - 2, base, 16, near[0]):
                copy.wait_recv()

        @pl.when((step >= 2) & (other == 0))
        def _():
            for copy in to_sibling(k, mine_at):
                copy.start()

        @pl.when(other == 1)
        def _():
            for copy in to_sibling(k, sib_at):
                copy.wait_recv()

        start = mine_at + other * (CHIPS + sib_at - mine_at)
        wide = blocks[pl.ds(start, UNIT)].astype(F32)
        first = wide[:, :COLS, :].reshape(UCOLS, HALF)
        second = wide[:, COLS:, :].reshape(UCOLS, HALF)
        cols = jnp.concatenate([first.astype(BF16), second.astype(BF16)], axis=1)
        spread = jnp.where(on_diagonal, jnp.broadcast_to(terms[pl.ds(start, UNIT)], (UNIT, COLS, 128)), 0.0)
        term_ = jnp.sum(spread, axis=2, keepdims=True).reshape(UCOLS, 1)
        for b in range(NX):
            lanes = slice(b * ROWS, (b + 1) * ROWS)
            cross = lax.dot_general(cols, x_buf[b], (((1,), (1,)), ((), ())), preferred_element_type=F32)
            scores = cross * (2.0 * KEEP * SCALE) + term_
            stash[pl.ds(start, UNIT), :, lanes] = scores.reshape(UNIT, COLS, ROWS)
            parts = scores.reshape(UCOLS // 8, 8, ROWS)
            old = row_m[:, lanes]
            top = jnp.maximum(old, jnp.max(parts, axis=0))
            row_m[:, lanes] = top
            row_s[:, lanes] = row_s[:, lanes] * jnp.exp2(old - top) + jnp.sum(
                jnp.exp2(parts - top[None]), axis=0
            )
        return 0

    lax.fori_loop(0, 8, row_unit, 0)

    m = row_m[...]
    top = jnp.max(m, axis=0, keepdims=True)
    total = jnp.sum(row_s[...] * jnp.exp2(m - top), axis=0, keepdims=True)
    row_l[x] = top + jnp.log2(total)
    for peer in x_peers:
        remote(row_l.at[x], row_l.at[x], row_send, row_recv, peer).start()
    gather_l = remote(row_l.at[pl.ds(0, 3)], row_l.at[pl.ds(0, 3)], row_send, row_recv, sibling)
    gather_l.wait_recv()
    parts = [row_l[b] for b in range(NX)]
    top = jnp.maximum(jnp.maximum(parts[0], parts[1]), jnp.maximum(parts[2], parts[3]))
    total = sum(jnp.exp2(part - top) for part in parts)
    whole = top + jnp.log2(total)
    for b in range(NX):
        send_l[b] = whole[:, b * ROWS : (b + 1) * ROWS]
    lifted = jnp.broadcast_to(whole, (8, NX * ROWS))

    def line_of(i):
        return (q + 4 + (i % 2) * ((i + 1) // 2) - (1 - i % 2) * (i // 2)) % 8

    def line_parts(q_, peak_ref, added_ref):
        for h in range(2):
            for j in range(8):
                at = slot_of(j, q_) if h == 0 else CHIPS + slot_of(q_, j)
                scores = stash[at].reshape(COLS // 8, 8, NX * ROWS) - lifted[None]
                pieces = [scores[:, :, i * 128 : (i + 1) * 128] for i in range(NX * ROWS // 128)]
                peak = pieces[0]
                for piece in pieces[1:]:
                    peak = jnp.maximum(peak, piece)
                added = jnp.exp2(pieces[0] - peak)
                for piece in pieces[1:]:
                    added = added + jnp.exp2(piece - peak)
                to = (h * 8 + j) * COLS
                peak_ref[to : to + COLS, :] = peak.reshape(COLS, 128)
                added_ref[to : to + COLS, :] = added.reshape(COLS, 128)

    def line_sums(peak_ref, added_ref):
        peak, added = jnp.transpose(peak_ref[...]), jnp.transpose(added_ref[...])
        crest = jnp.max(peak, axis=0, keepdims=True)
        return crest + jnp.log2(jnp.sum(added * jnp.exp2(peak - crest), axis=0, keepdims=True))

    def line_send(q_, peak_ref, added_ref):
        send_q[q_] = line_sums(peak_ref, added_ref)
        remote(send_q.at[q_], recv_q.at[q], q_send, q_recv, in_plane(p, q_)).start()

    a, b = (peak_a, added_a), (peak_b, added_b)
    line_parts(line_of(0), *a)

    def lines(i, _):
        line_parts(line_of(2 * i + 1), *b)
        line_send(line_of(2 * i), *a)
        line_parts(line_of(2 * i + 2), *a)
        line_send(line_of(2 * i + 1), *b)
        return 0

    lax.fori_loop(0, 3, lines, 0)
    line_parts(q, *b)
    line_send(line_of(6), *a)
    recv_q[q] = line_sums(*b)

    f_out[...] = sq_buf[...] * KEEP - (EPS * LN2) * send_l[x] + EPS * math.log(float(CHIPS * NX * NC * COLS))

    def combined(values):
        top = jnp.max(values, axis=0)
        return top + jnp.log2(jnp.sum(jnp.exp2(values - top[None]), axis=0))

    gather_q = remote(recv_q.at[pl.ds(0, 7)], recv_q.at[pl.ds(0, 7)], q_send, q_recv, sibling)
    gather_q.wait_recv()
    line = combined(recv_q[...])
    send_p[...] = line
    recv_p[p] = line
    for d in (4, 3, 5, 2, 6, 1, 7):
        remote(send_p, recv_p.at[p], p_send, p_recv, in_plane(p + d, q)).start()
    gather_p = remote(recv_p.at[pl.ds(0, 7)], recv_p.at[pl.ds(0, 7)], p_send, p_recv, sibling)
    gather_p.wait_recv()
    line = combined(recv_p[...])

    def segment(first):
        return sum(
            jnp.where(p == j, line[:, first + j * COLS : first + (j + 1) * COLS], 0.0) for j in range(8)
        )

    ours, theirs = segment(0), segment(8 * COLS)
    final[0] = jnp.concatenate([theirs, jnp.zeros((1, 128 - COLS), F32)], axis=1)
    swap = remote(final.at[0], final.at[1], fin_send, fin_recv, sibling)
    swap.start()
    swap.wait_recv()
    theirs = final[1][:, :COLS]
    top = jnp.maximum(ours, theirs)
    score = top + jnp.log2(jnp.exp2(ours - top) + jnp.exp2(theirs - top))
    g_out[...] = pot_buf[...] - (EPS * LN2) * score + EPS * (
        math.log(float(CHIPS * NX * NC * ROWS)) - math.log(float(CHIPS * NX * NC * COLS))
    )

    for copy in one + [gather_x, gather_l, gather_q, gather_p, swap] + outgoing:
        copy.wait_send()
    for k in range(4):
        for copy in to_sibling(k, 0):
            copy.wait_send()


def per_device(gen_samples, data_samples, data_potential):
    hbm = pl.BlockSpec(memory_space=pltpu.HBM)
    vmem = pl.BlockSpec(memory_space=pltpu.VMEM)
    dma = pltpu.SemaphoreType.DMA
    span = 2 * 8 * COLS
    f, g = pl.pallas_call(
        kernel,
        out_shape=(jax.ShapeDtypeStruct((1, ROWS), F32), jax.ShapeDtypeStruct((1, COLS), F32)),
        in_specs=[hbm, hbm, hbm],
        out_specs=(vmem, vmem),
        scratch_shapes=[
            pltpu.VMEM((NX, ROWS, WIDTH), BF16),
            pltpu.VMEM((COLS, WIDTH), BF16),
            pltpu.VMEM((1, COLS), F32),
            pltpu.VMEM((1, ROWS), F32),
            pltpu.VMEM((2 * CHIPS, 2 * COLS, HALF), BF16),
            pltpu.VMEM((2 * CHIPS, 1, 128), F32),
            pltpu.VMEM((2 * CHIPS, COLS, NX * ROWS), F32),
            pltpu.VMEM((8, NX * ROWS), F32),
            pltpu.VMEM((8, NX * ROWS), F32),
            pltpu.VMEM((NX, 1, NX * ROWS), F32),
            pltpu.VMEM((NX, 1, ROWS), F32),
            pltpu.VMEM((span, 128), F32),
            pltpu.VMEM((span, 128), F32),
            pltpu.VMEM((span, 128), F32),
            pltpu.VMEM((span, 128), F32),
            pltpu.VMEM((8, 1, span), F32),
            pltpu.VMEM((8, 1, span), F32),
            pltpu.VMEM((1, span), F32),
            pltpu.VMEM((8, 1, span), F32),
            pltpu.VMEM((2, 1, 128), F32),
            dma((3,)), dma, dma,
            dma((2,)), dma((2,)), dma((2, 4)), dma((2, 4)), dma((2, 4)), dma((2, 4)),
            dma, dma, dma, dma, dma, dma, dma, dma,
        ],
        compiler_params=pltpu.CompilerParams(
            collective_id=0, has_side_effects=True, vmem_limit_bytes=40 * 2**20
        ),
    )(*[
        pltpu.with_memory_space_constraint(array, pltpu.HBM)
        for array in (gen_samples, data_samples, data_potential.reshape(1, COLS))
    ])
    return f.reshape(ROWS), g.reshape(COLS)


def solution(mesh):
    in_specs = (P(("gen", "dat"), None), P(("dat", "gen"), None), P(("dat", "gen")))
    out_specs = (P(("gen", "dat")), P(("dat", "gen")))
    return jax.shard_map(
        per_device, mesh=mesh, in_specs=in_specs, out_specs=out_specs, check_vma=False
    )
```

time: 62 us -> 54.7 us (0.88)
  Pallas kernels: 57.8 us -> 52.9 us
  local copies, waits for them, and re-layouts: 3.33 us -> 1.08 us
    pallas_call x1, Pallas kernels: 57.8 us -> 52.9 us  [per_device(): pl.pallas_call(kernel, out_shape=(jax.ShapeDtypeStruct((1, ROWS), F32), j...]
    unnamed x8 -> x2, local copies, waits for them, and re-layouts: 3.33 us -> 1.08 us
where the time goes in v2:
time: 54.7 us; the launch traced here: 54.6 us
  Pallas kernels  52.9 us (97%)
  local copies, waits for them, and re-layouts  1.08 us (2%)
  between operations  0.64 us (1%)
    pallas_call x1, Pallas kernels, per_device(): pl.pallas_call(kernel, out_shape=(jax.ShapeDtypeStruct((1, ROWS), F32), j...  52.9 us

profile of v2, /device:TPU:1, one launch (start us, length us, event | category | flops | bytes accessed | tf_op | source)
XLA Modules:
  0.0 54.6 jit_solution(11020378418648842014)
XLA Ops:
  0.6 52.9 %shard_map.50 = (f32[1,256]{1,0:T(1,128)S(1)}, f32[1,24]{1,0:T(1,128)S(1)}) custom-call(bf16[256,256]{1,0:T(8,128)(2,1)} %gen_hbm.1, bf16[24,256]{1,0:T(8,128)(2,1)} %data_hbm.1, f32[1,24]{1,0:T(1,128)} %bitcast.5), custom_call_target="tpu_custom_call" | custom-call | tf_op jit(solution)/shard_map/pallas_call | solution.py:314
  53.5 0.6 %copy.7 = f32[256]{0:T(256)} copy(f32[256]{0:T(256)S(1)} %bitcast.3) | data formatting | bytes 2048
  54.1 0.5 copy.8

commit v3 on v2

--- a/solution.py
+++ b/solution.py
@@ -30,6 +30,8 @@
 def hops(d):
     return min(d % 8, -d % 8)
 
+
+FAR_FIRST = (4, 3, 5, 2, 6, 1, 7, 0)
 
 LATTICE = sorted(
     [(p, q) for q in range(8) for p in range(8) if (p + 2 * q) % 4 == 0 and (p, q) != (0, 0)],
@@ -52,9 +54,9 @@
 def kernel(
     gen_hbm, data_hbm, pot_hbm, f_out, g_out,
     x_buf, data_buf, pot_buf, sq_buf, blocks, terms, stash, row_m, row_s, row_l, send_l,
-    peak_a, added_a, peak_b, added_b, send_q, recv_q, send_p, recv_p, final,
+    peak_a, added_a, peak_b, added_b, send_c, recv_c, final,
     local_sem, x_send, x_recv, one_send, one_recv, two_send, two_recv, sib_send, sib_recv,
-    row_send, row_recv, q_send, q_recv, p_send, p_recv, fin_send, fin_recv,
+    row_send, row_recv, col_send, col_recv, fin_send, fin_recv,
 ):
     gen = lax.axis_index("gen")
     dat = lax.axis_index("dat")
@@ -133,20 +135,24 @@
             for i, ref in enumerate((blocks, terms))
         ]
 
-    def to_sibling(k, start):
+    def to_sibling(k, start, count):
         return [
-            remote(ref.at[pl.ds(start, 16)], ref.at[pl.ds(CHIPS + start, 16)], sib_send.at[i, k], sib_recv.at[i, k], sibling)
+            remote(
+                ref.at[pl.ds(start, count)], ref.at[pl.ds(CHIPS + start, count)],
+                sib_send.at[i, k], sib_recv.at[i, k], sibling,
+            )
             for i, ref in enumerate((blocks, terms))
         ]
 
-    base = kind * 16
+    base, sib_base = kind * 16, sib_kind * 16
     outgoing = (
-        to_near(2, base, 8, near[2]) + to_near(3, base + 8, 8, near[3])
-        + to_near(0, base, 16, near[0]) + to_near(1, base, 16, near[1])
+        to_near(0, base, 8, near[2]) + to_near(1, base + 8, 8, near[3])
+        + to_near(2, base, 8, near[0]) + to_near(3, base, 8, near[1])
+        + to_near(4, base + 8, 8, near[0]) + to_near(5, base + 8, 8, near[1])
     )
     for copy in outgoing:
         copy.start()
-    for copy in to_sibling(0, base):
+    for copy in to_sibling(0, base, 16):
         copy.start()
 
     gather_x = remote(x_buf.at[pl.ds(0, 3)], x_buf.at[pl.ds(0, 3)], x_send, x_recv, sibling)
@@ -159,31 +165,7 @@
     sub = lax.broadcasted_iota(jnp.int32, (UNIT, COLS, 128), 1)
     on_diagonal = lane == sub
 
-    def row_unit(step, _):
-        k, other = step // 2, step % 2
-        mine_at, sib_at = place(k, kind), place(k, sib_kind)
-
-        @pl.when(step == 2)
-        def _():
-            for copy in to_near(2, base, 8, near[2]) + to_near(3, base, 8, near[3]):
-                copy.wait_recv()
-
-        @pl.when((step >= 4) & (other == 0))
-        def _():
-            for copy in to_near(k - 2, base, 16, near[0]):
-                copy.wait_recv()
-
-        @pl.when((step >= 2) & (other == 0))
-        def _():
-            for copy in to_sibling(k, mine_at):
-                copy.start()
-
-        @pl.when(other == 1)
-        def _():
-            for copy in to_sibling(k, sib_at):
-                copy.wait_recv()
-
-        start = mine_at + other * (CHIPS + sib_at - mine_at)
+    def row_unit(start):
         wide = blocks[pl.ds(start, UNIT)].astype(F32)
         first = wide[:, :COLS, :].reshape(UCOLS, HALF)
         second = wide[:, COLS:, :].reshape(UCOLS, HALF)
@@ -202,9 +184,58 @@
             row_s[:, lanes] = row_s[:, lanes] * jnp.exp2(old - top) + jnp.sum(
                 jnp.exp2(parts - top[None]), axis=0
             )
+
+    def first_units(step, _):
+        @pl.when(step == 1)
+        def _():
+            for copy in to_sibling(0, sib_base, 16):
+                copy.wait_recv()
+
+        row_unit(base + step * (CHIPS + sib_base - base))
         return 0
 
-    lax.fori_loop(0, 8, row_unit, 0)
+    lax.fori_loop(0, 2, first_units, 0)
+
+    def next_units(step, _):
+        k, other = step % 3 + 1, step // 3
+        opposite, below, above = (place(i, kind) for i in (1, 2, 3))
+
+        @pl.when(step == 0)
+        def _():
+            for copy in to_near(0, opposite, 8, near[2]) + to_near(1, opposite, 8, near[3]):
+                copy.wait_recv()
+            for copy in to_sibling(1, opposite, 16):
+                copy.start()
+
+        @pl.when(step == 1)
+        def _():
+            for half in range(2):
+                for i, start in ((2, below), (3, above)):
+                    for copy in to_near(i + 2 * half, start, 8, near[0]):
+                        copy.wait_recv()
+                    for copy in to_sibling(i + 2 * half, start + 8 * half, 8):
+                        copy.start()
+
+        @pl.when(step == 3)
+        def _():
+            for copy in to_sibling(1, opposite, 16):
+                copy.wait_recv()
+
+        @pl.when(step == 4)
+        def _():
+            for copy in to_sibling(2, below, 8) + to_sibling(4, below, 8):
+                copy.wait_recv()
+
+        @pl.when(step == 5)
+        def _():
+            for copy in to_sibling(3, above, 8) + to_sibling(5, above, 8):
+                copy.wait_recv()
+
+        mine_at, sib_at = place(k, kind), place(k, sib_kind)
+        row_unit(mine_at + other * (CHIPS + sib_at - mine_at))
+        return 0
+
+    lax.fori_loop(0, 6, next_units, 0)
 
     m = row_m[...]
     top = jnp.max(m, axis=0, keepdims=True)
@@ -247,9 +278,11 @@
         return crest + jnp.log2(jnp.sum(added * jnp.exp2(peak - crest), axis=0, keepdims=True))
 
     def line_send(q_, peak_ref, added_ref):
-        send_q[q_] = line_sums(peak_ref, added_ref)
-        remote(send_q.at[q_], recv_q.at[q], q_send, q_recv, in_plane(p, q_)).start()
-
+        send_c[q_] = line_sums(peak_ref, added_ref)
+        for d in FAR_FIRST:
+            remote(send_c.at[q_], recv_c.at[here], col_send, col_recv, in_plane(p + d, q_)).start()
+
+    here = p * 8 + q
     a, b = (peak_a, added_a), (peak_b, added_b)
     line_parts(line_of(0), *a)
 
@@ -263,7 +296,11 @@
     lax.fori_loop(0, 3, lines, 0)
     line_parts(q, *b)
     line_send(line_of(6), *a)
-    recv_q[q] = line_sums(*b)
+    sums = line_sums(*b)
+    send_c[q] = sums
+    for d in FAR_FIRST[:-1]:
+        remote(send_c.at[q], recv_c.at[here], col_send, col_recv, in_plane(p + d, q)).start()
+    recv_c[here] = sums
 
     f_out[...] = sq_buf[...] * KEEP - (EPS * LN2) * send_l[x] + EPS * math.log(float(CHIPS * NX * NC * COLS))
 
@@ -271,16 +308,9 @@
         top = jnp.max(values, axis=0)
         return top + jnp.log2(jnp.sum(jnp.exp2(values - top[None]), axis=0))
 
-    gather_q = remote(recv_q.at[pl.ds(0, 7)], recv_q.at[pl.ds(0, 7)], q_send, q_recv, sibling)
-    gather_q.wait_recv()
-    line = combined(recv_q[...])
-    send_p[...] = line
-    recv_p[p] = line
-    for d in (4, 3, 5, 2, 6, 1, 7):
-        remote(send_p, recv_p.at[p], p_send, p_recv, in_plane(p + d, q)).start()
-    gather_p = remote(recv_p.at[pl.ds(0, 7)], recv_p.at[pl.ds(0, 7)], p_send, p_recv, sibling)
-    gather_p.wait_recv()
-    line = combined(recv_p[...])
+    gather_c = remote(recv_c.at[pl.ds(0, CHIPS - 1)], recv_c.at[pl.ds(0, CHIPS - 1)], col_send, col_recv, sibling)
+    gather_c.wait_recv()
+    line = combined(recv_c[...])
 
     def segment(first):
         return sum(
@@ -299,10 +329,10 @@
         math.log(float(CHIPS * NX * NC * ROWS)) - math.log(float(CHIPS * NX * NC * COLS))
     )
 
-    for copy in one + [gather_x, gather_l, gather_q, gather_p, swap] + outgoing:
+    for copy in one + [gather_x, gather_l, gather_c, swap] + outgoing:
         copy.wait_send()
-    for k in range(4):
-        for copy in to_sibling(k, 0):
+    for k, count in enumerate((16, 16, 8, 8, 8, 8)):
+        for copy in to_sibling(k, 0, count):
             copy.wait_send()
 
 
@@ -333,13 +363,11 @@
             pltpu.VMEM((span, 128), F32),
             pltpu.VMEM((span, 128), F32),
             pltpu.VMEM((8, 1, span), F32),
-            pltpu.VMEM((8, 1, span), F32),
-            pltpu.VMEM((1, span), F32),
-            pltpu.VMEM((8, 1, span), F32),
+            pltpu.VMEM((CHIPS, 1, span), F32),
             pltpu.VMEM((2, 1, 128), F32),
             dma((3,)), dma, dma,
-            dma((2,)), dma((2,)), dma((2, 4)), dma((2, 4)), dma((2, 4)), dma((2, 4)),
-            dma, dma, dma, dma, dma, dma, dma, dma,
+            dma((2,)), dma((2,)), dma((2, 6)), dma((2, 6)), dma((2, 6)), dma((2, 6)),
+            dma, dma, dma, dma, dma, dma,
         ],
         compiler_params=pltpu.CompilerParams(
             collective_id=0, has_side_effects=True, vmem_limit_bytes=40 * 2**20

time: 54.7 us -> 52.7 us (0.963)
  Pallas kernels: 52.9 us -> 50.8 us
    pallas_call x1, Pallas kernels: 52.9 us -> 50.8 us  [per_device(): pl.pallas_call(kernel, out_shape=(jax.ShapeDtypeStruct((1, ROWS), F32), j...]
where the time goes in v3:
time: 52.7 us; the launch traced here: 52.5 us
  Pallas kernels  50.8 us (96%)
  local copies, waits for them, and re-layouts  1.08 us (2%)
  between operations  0.64 us (1%)
    pallas_call x1, Pallas kernels, per_device(): pl.pallas_call(kernel, out_shape=(jax.ShapeDtypeStruct((1, ROWS), F32), j...  50.8 us
    unnamed x2, local copies, waits for them, and re-layouts  1.08 us

profile of v3, /device:TPU:1, one launch (start us, length us, event | category | flops | bytes accessed | tf_op | source)
XLA Modules:
  0.0 52.5 jit_solution(8783929009490771193)
XLA Ops:
  0.6 50.8 %shard_map.50 = (f32[1,256]{1,0:T(1,128)S(1)}, f32[1,24]{1,0:T(1,128)S(1)}) custom-call(bf16[256,256]{1,0:T(8,128)(2,1)} %gen_hbm.1, bf16[24,256]{1,0:T(8,128)(2,1)} %data_hbm.1, f32[1,24]{1,0:T(1,128)} %bitcast.5), custom_call_target="tpu_custom_call" | custom-call | tf_op jit(solution)/shard_map/pallas_call | solution.py:344
  51.4 0.6 %copy.7 = f32[256]{0:T(256)} copy(f32[256]{0:T(256)S(1)} %bitcast.3) | data formatting | bytes 2048
  52.0 0.5 copy.8

commit v4 on v3

v4 whole, which is shorter than its diff:
```python
import math

import jax
import jax.numpy as jnp
from jax import lax
from jax.experimental import pallas as pl
from jax.experimental.pallas import tpu as pltpu
from jax.sharding import PartitionSpec as P

EPS = 0.05
LOG2E = math.log2(math.e)
LN2 = math.log(2.0)
SCALE = LOG2E / EPS
LOW = -1e30
MESH = pl.DeviceIdType.MESH
F32 = jnp.float32
BF16 = jnp.bfloat16

NX, NY, NZ, NC = 4, 8, 8, 2
CHIPS = NY * NZ
ROWS = 256
COLS = 24
WIDTH = 256
HALF = WIDTH // 2
KEEP = 1.0 / WIDTH


def hops(d):
    return min(d % 8, -d % 8)


FAR_FIRST = (4, 3, 5, 2, 6, 1, 7, 0)

NEAR0 = [(0, 0), (0, 2), (0, -2), (2, 1), (2, -1), (-2, 1), (-2, -1), (0, 4)]
FAR0 = [(4, 0), (2, 3), (2, -3), (-2, 3), (-2, -3), (4, 2), (4, -2), (4, 4)]
NEAR2 = ([(0, 1), (2, 2), (-2, 2), (2, 0)], [(0, -1), (2, -2), (-2, -2), (-2, 0)])
FAR2 = ([(0, 3), (4, 1), (4, 3), (2, 4)], [(0, -3), (4, -1), (4, -3), (-2, 4)])


def shifted(offsets, dp, dq):
    return [(a + dp, b + dq) for a, b in offsets]


ORDER = (
    NEAR0 + FAR0
    + shifted(NEAR0, 1, 0) + NEAR2[0] + NEAR2[1] + shifted(NEAR0, -1, 0)
    + shifted(FAR0, 1, 0) + FAR2[0] + FAR2[1] + shifted(FAR0, -1, 0)
)
SLOT = {(a % 8, b % 8): slot for slot, (a, b) in enumerate(ORDER)}


def slot_of(dp, dq):
    return SLOT[dp % 8, dq % 8]


def squares(values):
    wide = values.astype(F32)
    wide = wide * wide
    high = wide.astype(BF16)
    low = (wide - high.astype(F32)).astype(BF16)
    ones = jnp.ones((8, WIDTH), BF16)
    dims = (((1,), (1,)), ((), ()))
    return lax.dot_general(ones, high, dims, preferred_element_type=F32) + lax.dot_general(
        ones, low, dims, preferred_element_type=F32
    )


def kernel(
    gen_hbm, data_hbm, pot_hbm, f_out, g_out,
    x_buf, data_buf, pot_buf, sq_buf, blocks, terms, stash, row_m, row_s, row_l, send_l,
    peak_a, added_a, peak_b, added_b, send_c, recv_c, final,
    local_sem, x_send, x_recv, one_send, one_recv, two_send, two_recv, sib_send, sib_recv,
    row_send, row_recv, col_send, col_recv, fin_send, fin_recv,
):
    gen = lax.axis_index("gen")
    dat = lax.axis_index("dat")
    x, c = (dat // 2) % NX, dat % 2
    y, z = (dat // 8) * 4 + gen % 4, gen // 4

    def device(x_, y_, z_, c_):
        return (z_ * 4 + y_ % 4, (y_ // 4) * 8 + x_ * 2 + c_)

    p, q = y + c * (z - y), z + c * (y - z)

    def in_plane(p_, q_):
        p_, q_ = p_ % 8, q_ % 8
        return device(x, p_ + c * (q_ - p_), q_ + c * (p_ - q_), c)

    sibling = device(x, y, z, 1 - c)
    x_peers = [device((x + d) % NX, y, z, c) for d in (2, 1, 3)]
    near = [in_plane(p + 1, q), in_plane(p - 1, q), in_plane(p, q + 1), in_plane(p, q - 1)]
    group = [in_plane(p + dp, q + dq) for dp, dq in reversed((NEAR0 + FAR0)[1:])]

    loads = [
        pltpu.make_async_copy(data_hbm, data_buf, local_sem.at[0]),
        pltpu.make_async_copy(pot_hbm, pot_buf, local_sem.at[1]),
        pltpu.make_async_copy(gen_hbm, x_buf.at[x], local_sem.at[2]),
    ]
    for copy in loads:
        copy.start()

    peers = group + near + x_peers + [sibling]
    barrier = pltpu.get_barrier_semaphore()
    for peer in peers:
        pl.semaphore_signal(barrier, inc=1, device_id=peer, device_id_type=MESH)

    for copy in loads[:2]:
        copy.wait()
    data = data_buf[...].astype(F32)
    blocks[0] = jnp.concatenate([data[:, :HALF], data[:, HALF:]], axis=0).astype(BF16)
    term = (pot_buf[...] - squares(data_buf[...])[0:1, :] * KEEP) * SCALE
    terms[0] = jnp.concatenate([term, jnp.zeros((1, 128 - COLS), F32)], axis=1)

    pl.semaphore_wait(barrier, len(peers))

    def remote(src, dst, send, recv, peer):
        return pltpu.make_async_remote_copy(
            src_ref=src, dst_ref=dst, send_sem=send, recv_sem=recv, device_id=peer, device_id_type=MESH
        )

    def to_group(i, ref):
        for dp, dq in reversed((NEAR0 + FAR0)[1:]):
            far = int((dp, dq) in FAR0)
            remote(
                ref.at[0], ref.at[slot_of(dp, dq)], one_send.at[i, far], one_recv.at[i, far], in_plane(p - dp, q - dq)
            ).start()

    to_group(0, blocks)
    for peer in x_peers:
        remote(gen_hbm, x_buf.at[x], x_send, x_recv, peer).start()
    to_group(1, terms)

    row_m[...] = jnp.full(row_m.shape, LOW, F32)
    row_s[...] = jnp.zeros(row_s.shape, F32)
    loads[2].wait()
    sq_buf[...] = squares(x_buf[x])[0:1, :]

    refs = (blocks, terms)

    def from_group(far):
        return [
            remote(ref.at[pl.ds(0, 7 + far)], ref.at[pl.ds(0, 7 + far)], one_send.at[i, far], one_recv.at[i, far], sibling)
            for i, ref in enumerate(refs)
        ]

    def to_near(k, far, count, src, dst, peer):
        return [
            remote(
                ref.at[pl.ds(src, count)], ref.at[pl.ds(dst, count)],
                two_send.at[i, k, far], two_recv.at[i, k, far], peer,
            )
            for i, ref in enumerate(refs)
        ]

    def send_near(far):
        first = 16 + 24 * far
        for k, slots in ((0, first), (1, first + 16)):
            for copy in to_near(k, far, 8, 8 * far, slots, near[1 - k]):
                copy.start()
        for side, ways in enumerate((NEAR2, FAR2)[far]):
            for dp, dq in ways:
                held = slot_of(dp, dq + 2 * side - 1)
                for copy in to_near(2 + side, far, 1, held, slot_of(dp, dq), near[3 - side]):
                    copy.start()

    def from_near(far):
        counts = (8, 8, 4, 4)
        return sum((to_near(k, far, count, 0, 0, sibling) for k, count in enumerate(counts)), [])

    def to_sibling(k, start, count):
        return [
            remote(
                ref.at[pl.ds(start, count)], ref.at[pl.ds(CHIPS + start, count)],
                sib_send.at[i, k], sib_recv.at[i, k], sibling,
            )
            for i, ref in enumerate(refs)
        ]

    passed_on = [to_sibling(0, 0, 8), to_sibling(1, 8, 8), to_sibling(2, 16, 24), to_sibling(3, 40, 24)]
    for far in range(2):
        for copy in from_group(far):
            copy.wait_recv()
        send_near(far)
        for copy in passed_on[far]:
            copy.start()

    gather_x = remote(x_buf.at[pl.ds(0, 3)], x_buf.at[pl.ds(0, 3)], x_send, x_recv, sibling)
    gather_x.wait_recv()

    def row_unit(start, count):
        wide = blocks[pl.ds(start, count)].astype(F32)
        first = wide[:, :COLS, :].reshape(count * COLS, HALF)
        second = wide[:, COLS:, :].reshape(count * COLS, HALF)
        cols = jnp.concatenate([first.astype(BF16), second.astype(BF16)], axis=1)
        shape = (count, COLS, 128)
        on_diagonal = lax.broadcasted_iota(jnp.int32, shape, 2) == lax.broadcasted_iota(jnp.int32, shape, 1)
        spread = jnp.where(on_diagonal, jnp.broadcast_to(terms[pl.ds(start, count)], shape), 0.0)
        term_ = jnp.sum(spread, axis=2, keepdims=True).reshape(count * COLS, 1)
        for b in range(NX):
            lanes = slice(b * ROWS, (b + 1) * ROWS)
            cross = lax.dot_general(cols, x_buf[b], (((1,), (1,)), ((), ())), preferred_element_type=F32)
            scores = cross * (2.0 * KEEP * SCALE) + term_
            stash[pl.ds(start, count), :, lanes] = scores.reshape(count, COLS, ROWS)
            parts = scores.reshape(count * COLS // 8, 8, ROWS)
            old = row_m[:, lanes]
            top = jnp.maximum(old, jnp.max(parts, axis=0))
            row_m[:, lanes] = top
            row_s[:, lanes] = row_s[:, lanes] * jnp.exp2(old - top) + jnp.sum(
                jnp.exp2(parts - top[None]), axis=0
            )

    def first_units(step, _):
        @pl.when(step == 1)
        def _():
            for copy in from_near(0):
                copy.wait_recv()
            for copy in passed_on[2]:
                copy.start()
            for copy in passed_on[0] + passed_on[1]:
                copy.wait_recv()

        row_unit(CHIPS * step, 16)
        return 0

    lax.fori_loop(0, 2, first_units, 0)

    def next_units(step, _):
        @pl.when(step == 1)
        def _():
            for copy in passed_on[2]:
                copy.wait_recv()

        @pl.when(step == 2)
        def _():
            for copy in from_near(1):
                copy.wait_recv()
            for copy in passed_on[3]:
                copy.start()

        @pl.when(step == 3)
        def _():
            for copy in passed_on[3]:
                copy.wait_recv()

        row_unit(16 + 24 * (step // 2) + CHIPS * (step % 2), 24)
        return 0

    lax.fori_loop(0, 4, next_units, 0)

    m = row_m[...]
    top = jnp.max(m, axis=0, keepdims=True)
    total = jnp.sum(row_s[...] * jnp.exp2(m - top), axis=0, keepdims=True)
    row_l[x] = top + jnp.log2(total)
    for peer in x_peers:
        remote(row_l.at[x], row_l.at[x], row_send, row_recv, peer).start()
    gather_l = remote(row_l.at[pl.ds(0, 3)], row_l.at[pl.ds(0, 3)], row_send, row_recv, sibling)
    gather_l.wait_recv()
    parts = [row_l[b] for b in range(NX)]
    top = jnp.maximum(jnp.maximum(parts[0], parts[1]), jnp.maximum(parts[2], parts[3]))
    total = sum(jnp.exp2(part - top) for part in parts)
    whole = top + jnp.log2(total)
    for b in range(NX):
        send_l[b] = whole[:, b * ROWS : (b + 1) * ROWS]
    lifted = jnp.broadcast_to(whole, (8, NX * ROWS))

    def line_parts(dq, peak_ref, added_ref):
        for h in range(2):
            for j in range(8):
                at = slot_of(j, dq) if h == 0 else CHIPS + slot_of(dq, j)
                scores = stash[at].reshape(COLS // 8, 8, NX * ROWS) - lifted[None]
                pieces = [scores[:, :, i * 128 : (i + 1) * 128] for i in range(NX * ROWS // 128)]
                peak = pieces[0]
                for piece in pieces[1:]:
                    peak = jnp.maximum(peak, piece)
                added = jnp.exp2(pieces[0] - peak)
                for piece in pieces[1:]:
                    added = added + jnp.exp2(piece - peak)
                to = (h * 8 + j) * COLS
                peak_ref[to : to + COLS, :] = peak.reshape(COLS, 128)
                added_ref[to : to + COLS, :] = added.reshape(COLS, 128)

    def line_sums(peak_ref, added_ref):
        peak, added = jnp.transpose(peak_ref[...]), jnp.transpose(added_ref[...])
        crest = jnp.max(peak, axis=0, keepdims=True)
        return crest + jnp.log2(jnp.sum(added * jnp.exp2(peak - crest), axis=0, keepdims=True))

    def line_send(dq, peak_ref, added_ref):
        sums = line_sums(peak_ref, added_ref)
        send_c[dq] = sums
        for dp in FAR_FIRST:
            if (dp, dq) == (0, 0):
                recv_c[0] = sums
            else:
                seen = (-dp % 8) * 8 + -dq % 8
                remote(send_c.at[dq], recv_c.at[seen], col_send, col_recv, in_plane(p + dp, q + dq)).start()

    room = ((peak_a, added_a), (peak_b, added_b))
    line_parts(FAR_FIRST[0], *room[0])
    for i in range(8):
        if i < 7:
            line_parts(FAR_FIRST[i + 1], *room[(i + 1) % 2])
        line_send(FAR_FIRST[i], *room[i % 2])

    f_out[...] = sq_buf[...] * KEEP - (EPS * LN2) * send_l[x] + EPS * math.log(float(CHIPS * NX * NC * COLS))

    def combined(values):
        top = jnp.max(values, axis=0)
        return top + jnp.log2(jnp.sum(jnp.exp2(values - top[None]), axis=0))

    gather_c = remote(recv_c.at[pl.ds(0, CHIPS - 1)], recv_c.at[pl.ds(0, CHIPS - 1)], col_send, col_recv, sibling)
    gather_c.wait_recv()

    sums = [combined(recv_c[pl.ds(8 * dp, 8)]) for dp in range(8)]

    def segment(first):
        parts = [sums[dp][:, first + (-dp % 8) * COLS :][:, :COLS] for dp in range(8)]
        top = parts[0]
        for part in parts[1:]:
            top = jnp.maximum(top, part)
        return top + jnp.log2(sum(jnp.exp2(part - top) for part in parts))

    ours, theirs = segment(0), segment(8 * COLS)
    final[0] = jnp.concatenate([theirs, jnp.zeros((1, 128 - COLS), F32)], axis=1)
    swap = remote(final.at[0], final.at[1], fin_send, fin_recv, sibling)
    swap.start()
    swap.wait_recv()
    theirs = final[1][:, :COLS]
    top = jnp.maximum(ours, theirs)
    score = top + jnp.log2(jnp.exp2(ours - top) + jnp.exp2(theirs - top))
    g_out[...] = pot_buf[...] - (EPS * LN2) * score + EPS * (
        math.log(float(CHIPS * NX * NC * ROWS)) - math.log(float(CHIPS * NX * NC * COLS))
    )

    for copy in [gather_x, gather_l, gather_c, swap]:
        copy.wait_send()
    for far in range(2):
        for copy in from_group(far) + from_near(far):
            copy.wait_send()
    for copy in sum(passed_on, []):
        copy.wait_send()


def per_device(gen_samples, data_samples, data_potential):
    hbm = pl.BlockSpec(memory_space=pltpu.HBM)
    vmem = pl.BlockSpec(memory_space=pltpu.VMEM)
    dma = pltpu.SemaphoreType.DMA
    span = 2 * 8 * COLS
    f, g = pl.pallas_call(
        kernel,
        out_shape=(jax.ShapeDtypeStruct((1, ROWS), F32), jax.ShapeDtypeStruct((1, COLS), F32)),
        in_specs=[hbm, hbm, hbm],
        out_specs=(vmem, vmem),
        scratch_shapes=[
            pltpu.VMEM((NX, ROWS, WIDTH), BF16),
            pltpu.VMEM((COLS, WIDTH), BF16),
            pltpu.VMEM((1, COLS), F32),
            pltpu.VMEM((1, ROWS), F32),
            pltpu.VMEM((2 * CHIPS, 2 * COLS, HALF), BF16),
            pltpu.VMEM((2 * CHIPS, 1, 128), F32),
            pltpu.VMEM((2 * CHIPS, COLS, NX * ROWS), F32),
            pltpu.VMEM((8, NX * ROWS), F32),
            pltpu.VMEM((8, NX * ROWS), F32),
            pltpu.VMEM((NX, 1, NX * ROWS), F32),
            pltpu.VMEM((NX, 1, ROWS), F32),
            pltpu.VMEM((span, 128), F32),
            pltpu.VMEM((span, 128), F32),
            pltpu.VMEM((span, 128), F32),
            pltpu.VMEM((span, 128), F32),
            pltpu.VMEM((8, 1, span), F32),
            pltpu.VMEM((CHIPS, 1, span), F32),
            pltpu.VMEM((2, 1, 128), F32),
            dma((3,)), dma, dma,
            dma((2, 2)), dma((2, 2)), dma((2, 4, 2)), dma((2, 4, 2)), dma((2, 4)), dma((2, 4)),
            dma, dma, dma, dma, dma, dma,
        ],
        compiler_params=pltpu.CompilerParams(
            collective_id=0, has_side_effects=True, vmem_limit_bytes=40 * 2**20
        ),
    )(*[
        pltpu.with_memory_space_constraint(array, pltpu.HBM)
        for array in (gen_samples, data_samples, data_potential.reshape(1, COLS))
    ])
    return f.reshape(ROWS), g.reshape(COLS)


def solution(mesh):
    in_specs = (P(("gen", "dat"), None), P(("dat", "gen"), None), P(("dat", "gen")))
    out_specs = (P(("gen", "dat")), P(("dat", "gen")))
    return jax.shard_map(
        per_device, mesh=mesh, in_specs=in_specs, out_specs=out_specs, check_vma=False
    )
```

time: 52.7 us -> 49.5 us (0.939)
  Pallas kernels: 50.8 us -> 47.6 us
    pallas_call x1, Pallas kernels: 50.8 us -> 47.6 us  [per_device(): pl.pallas_call(kernel, out_shape=(jax.ShapeDtypeStruct((1, ROWS), F32), j...]
where the time goes in v4:
time: 49.5 us; the launch traced here: 49.3 us
  Pallas kernels  47.6 us (96%)
  local copies, waits for them, and re-layouts  1.08 us (2%)
  between operations  0.64 us (1%)
    pallas_call x1, Pallas kernels, per_device(): pl.pallas_call(kernel, out_shape=(jax.ShapeDtypeStruct((1, ROWS), F32), j...  47.6 us
    unnamed x2, local copies, waits for them, and re-layouts  1.08 us

profile of v4, /device:TPU:1, one launch (start us, length us, event | category | flops | bytes accessed | tf_op | source)
XLA Modules:
  0.0 49.3 jit_solution(16241763708182897029)
XLA Ops:
  0.6 47.6 %shard_map.50 = (f32[1,256]{1,0:T(1,128)S(1)}, f32[1,24]{1,0:T(1,128)S(1)}) custom-call(bf16[256,256]{1,0:T(8,128)(2,1)} %gen_hbm.1, bf16[24,256]{1,0:T(8,128)(2,1)} %data_hbm.1, f32[1,24]{1,0:T(1,128)} %bitcast.5), custom_call_target="tpu_custom_call" | custom-call | tf_op jit(solution)/shard_map/pallas_call | solution.py:348
  48.2 0.6 %copy.7 = f32[256]{0:T(256)} copy(f32[256]{0:T(256)S(1)} %bitcast.3) | data formatting | bytes 2048
  48.8 0.5 %copy.8 = f32[24]{0:T(128)} copy(f32[24]{0:T(128)S(1)} %bitcast.4) | data formatting | bytes 192

commit v5 on v4

--- a/solution.py
+++ b/solution.py
@@ -22,6 +22,7 @@
 COLS = 24
 WIDTH = 256
 HALF = WIDTH // 2
+LINE = 8 * NC * COLS
 KEEP = 1.0 / WIDTH
 
 
@@ -68,7 +69,7 @@
 def kernel(
     gen_hbm, data_hbm, pot_hbm, f_out, g_out,
     x_buf, data_buf, pot_buf, sq_buf, blocks, terms, stash, row_m, row_s, row_l, send_l,
-    peak_a, added_a, peak_b, added_b, send_c, recv_c, final,
+    line_a, line_b, send_c, recv_c, final,
     local_sem, x_send, x_recv, one_send, one_recv, two_send, two_recv, sib_send, sib_recv,
     row_send, row_recv, col_send, col_recv, fin_send, fin_recv,
 ):
@@ -263,7 +264,7 @@
         send_l[b] = whole[:, b * ROWS : (b + 1) * ROWS]
     lifted = jnp.broadcast_to(whole, (8, NX * ROWS))
 
-    def line_parts(dq, peak_ref, added_ref):
+    def line_parts(dq, line_ref):
         for h in range(2):
             for j in range(8):
                 at = slot_of(j, dq) if h == 0 else CHIPS + slot_of(dq, j)
@@ -275,51 +276,63 @@
                 added = jnp.exp2(pieces[0] - peak)
                 for piece in pieces[1:]:
                     added = added + jnp.exp2(piece - peak)
-                to = (h * 8 + j) * COLS
-                peak_ref[to : to + COLS, :] = peak.reshape(COLS, 128)
-                added_ref[to : to + COLS, :] = added.reshape(COLS, 128)
-
-    def line_sums(peak_ref, added_ref):
-        peak, added = jnp.transpose(peak_ref[...]), jnp.transpose(added_ref[...])
-        crest = jnp.max(peak, axis=0, keepdims=True)
-        return crest + jnp.log2(jnp.sum(added * jnp.exp2(peak - crest), axis=0, keepdims=True))
-
-    def line_send(dq, peak_ref, added_ref):
-        sums = line_sums(peak_ref, added_ref)
-        send_c[dq] = sums
-        for dp in FAR_FIRST:
-            if (dp, dq) == (0, 0):
-                recv_c[0] = sums
-            else:
-                seen = (-dp % 8) * 8 + -dq % 8
-                remote(send_c.at[dq], recv_c.at[seen], col_send, col_recv, in_plane(p + dp, q + dq)).start()
-
-    room = ((peak_a, added_a), (peak_b, added_b))
-    line_parts(FAR_FIRST[0], *room[0])
-    for i in range(8):
-        if i < 7:
-            line_parts(FAR_FIRST[i + 1], *room[(i + 1) % 2])
-        line_send(FAR_FIRST[i], *room[i % 2])
-
-    f_out[...] = sq_buf[...] * KEEP - (EPS * LN2) * send_l[x] + EPS * math.log(float(CHIPS * NX * NC * COLS))
+                to = (2 * j + h) * COLS
+                line_ref[to : to + COLS, :] = (peak + jnp.log2(added)).reshape(COLS, 128)
 
     def combined(values):
         top = jnp.max(values, axis=0)
         return top + jnp.log2(jnp.sum(jnp.exp2(values - top[None]), axis=0))
 
-    gather_c = remote(recv_c.at[pl.ds(0, CHIPS - 1)], recv_c.at[pl.ds(0, CHIPS - 1)], col_send, col_recv, sibling)
+    def tiles_of(j):
+        first = 2 * COLS * j // 128
+        return first, (2 * COLS * (j + 1) - 1) // 128 - first + 1
+
+    def line_send(dq, line_ref):
+        values = jnp.transpose(line_ref[...])
+        top = jnp.max(values, axis=0, keepdims=True)
+        sums = top + jnp.log2(jnp.sum(jnp.exp2(values - top), axis=0, keepdims=True))
+        for t in range(LINE // 128):
+            send_c[dq, t] = sums[:, 128 * t : 128 * (t + 1)]
+        for dp in FAR_FIRST:
+            first, count = tiles_of(dp)
+            if (dp, dq) == (0, 0):
+                recv_c[0] = sums[:, :128]
+            else:
+                seen = 2 * ((-dp % 8) * 8 + -dq % 8)
+                remote(
+                    send_c.at[dq, pl.ds(first, count)], recv_c.at[pl.ds(seen, count)],
+                    col_send, col_recv, in_plane(p + dp, q + dq),
+                ).start()
+
+    room = (line_a, line_b)
+    line_parts(FAR_FIRST[0], room[0])
+    for i in range(8):
+        if i < 7:
+            line_parts(FAR_FIRST[i + 1], room[(i + 1) % 2])
+        line_send(FAR_FIRST[i], room[i % 2])
+
+    f_out[...] = sq_buf[...] * KEEP - (EPS * LN2) * send_l[x] + EPS * math.log(float(CHIPS * NX * NC * COLS))
+
+    tiles = 8 * sum(tiles_of(j)[1] for j in range(8)) - 1
+    gather_c = remote(recv_c.at[pl.ds(0, tiles)], recv_c.at[pl.ds(0, tiles)], col_send, col_recv, sibling)
     gather_c.wait_recv()
 
-    sums = [combined(recv_c[pl.ds(8 * dp, 8)]) for dp in range(8)]
-
-    def segment(first):
-        parts = [sums[dp][:, first + (-dp % 8) * COLS :][:, :COLS] for dp in range(8)]
-        top = parts[0]
-        for part in parts[1:]:
-            top = jnp.maximum(top, part)
-        return top + jnp.log2(sum(jnp.exp2(part - top) for part in parts))
-
-    ours, theirs = segment(0), segment(8 * COLS)
+    parts = []
+    for dp in range(8):
+        j = -dp % 8
+        first, count = tiles_of(j)
+        tiles = [
+            combined(jnp.concatenate([recv_c[pl.ds(2 * (8 * dp + dq) + t, 1)] for dq in range(8)], axis=0))
+            for t in range(count)
+        ]
+        row = jnp.concatenate(tiles, axis=1)
+        start = 2 * COLS * j - 128 * first
+        parts.append(row[:, start : start + 2 * COLS])
+    top = parts[0]
+    for part in parts[1:]:
+        top = jnp.maximum(top, part)
+    both = top + jnp.log2(sum(jnp.exp2(part - top) for part in parts))
+    ours, theirs = both[:, :COLS], both[:, COLS:]
     final[0] = jnp.concatenate([theirs, jnp.zeros((1, 128 - COLS), F32)], axis=1)
     swap = remote(final.at[0], final.at[1], fin_send, fin_recv, sibling)
     swap.start()
@@ -344,7 +357,6 @@
     hbm = pl.BlockSpec(memory_space=pltpu.HBM)
     vmem = pl.BlockSpec(memory_space=pltpu.VMEM)
     dma = pltpu.SemaphoreType.DMA
-    span = 2 * 8 * COLS
     f, g = pl.pallas_call(
         kernel,
         out_shape=(jax.ShapeDtypeStruct((1, ROWS), F32), jax.ShapeDtypeStruct((1, COLS), F32)),
@@ -362,12 +374,10 @@
             pltpu.VMEM((8, NX * ROWS), F32),
             pltpu.VMEM((NX, 1, NX * ROWS), F32),
             pltpu.VMEM((NX, 1, ROWS), F32),
-            pltpu.VMEM((span, 128), F32),
-            pltpu.VMEM((span, 128), F32),
-            pltpu.VMEM((span, 128), F32),
-            pltpu.VMEM((span, 128), F32),
-            pltpu.VMEM((8, 1, span), F32),
-            pltpu.VMEM((CHIPS, 1, span), F32),
+            pltpu.VMEM((LINE, 128), F32),
+            pltpu.VMEM((LINE, 128), F32),
+            pltpu.VMEM((8, LINE // 128, 1, 128), F32),
+            pltpu.VMEM((2 * CHIPS, 1, 128), F32),
             pltpu.VMEM((2, 1, 128), F32),
             dma((3,)), dma, dma,
             dma((2, 2)), dma((2, 2)), dma((2, 4, 2)), dma((2, 4, 2)), dma((2, 4)), dma((2, 4)),

time: 49.5 us -> 49.7 us (level)
  no operation moved by 1% of the time
where the time goes in v5:
time: 49.7 us; the launch traced here: 49.5 us
  Pallas kernels  47.8 us (96%)
  local copies, waits for them, and re-layouts  1.08 us (2%)
  between operations  0.64 us (1%)
    pallas_call x1, Pallas kernels, per_device(): pl.pallas_call(kernel, out_shape=(jax.ShapeDtypeStruct((1, ROWS), F32), j...  47.8 us
    unnamed x2, local copies, waits for them, and re-layouts  1.08 us

profile of v5, /device:TPU:1, one launch (start us, length us, event | category | flops | bytes accessed | tf_op | source)
XLA Modules:
  0.0 49.5 jit_solution(2169998318325170597)
XLA Ops:
  0.6 47.8 %shard_map.50 = (f32[1,256]{1,0:T(1,128)S(1)}, f32[1,24]{1,0:T(1,128)S(1)}) custom-call(bf16[256,256]{1,0:T(8,128)(2,1)} %gen_hbm.1, bf16[24,256]{1,0:T(8,128)(2,1)} %data_hbm.1, f32[1,24]{1,0:T(1,128)} %bitcast.5), custom_call_target="tpu_custom_call" | custom-call | tf_op jit(solution)/shard_map/pallas_call | solution.py:360
  48.4 0.6 %copy.7 = f32[256]{0:T(256)} copy(f32[256]{0:T(256)S(1)} %bitcast.3) | data formatting | bytes 2048
  49.0 0.5 %copy.8 = f32[24]{0:T(128)} copy(f32[24]{0:T(128)S(1)} %bitcast.4) | data formatting | bytes 192

commit v6 on v5

--- a/solution.py
+++ b/solution.py
@@ -33,21 +33,39 @@
 FAR_FIRST = (4, 3, 5, 2, 6, 1, 7, 0)
 
 NEAR0 = [(0, 0), (0, 2), (0, -2), (2, 1), (2, -1), (-2, 1), (-2, -1), (0, 4)]
-FAR0 = [(4, 0), (2, 3), (2, -3), (-2, 3), (-2, -3), (4, 2), (4, -2), (4, 4)]
+FAR0 = [(4, 0), (2, 3), (2, -3), (-2, 3), (-2, -3)]
 NEAR2 = ([(0, 1), (2, 2), (-2, 2), (2, 0)], [(0, -1), (2, -2), (-2, -2), (-2, 0)])
-FAR2 = ([(0, 3), (4, 1), (4, 3), (2, 4)], [(0, -3), (4, -1), (4, -3), (-2, 4)])
+FAR2 = ([(0, 3), (4, 1), (2, 4)], [(0, -3), (4, -1), (-2, 4)])
 
 
 def shifted(offsets, dp, dq):
     return [(a + dp, b + dq) for a, b in offsets]
 
 
+def folded(offset):
+    return tuple((d + 3) % 8 - 3 for d in offset)
+
+
+FIRST = NEAR0 + FAR0
 ORDER = (
-    NEAR0 + FAR0
-    + shifted(NEAR0, 1, 0) + NEAR2[0] + NEAR2[1] + shifted(NEAR0, -1, 0)
-    + shifted(FAR0, 1, 0) + FAR2[0] + FAR2[1] + shifted(FAR0, -1, 0)
+    FIRST
+    + shifted(NEAR0, 1, 0) + shifted(NEAR0, -1, 0) + NEAR2[0] + NEAR2[1]
+    + shifted(FAR0, 1, 0) + shifted(FAR0, -1, 0) + FAR2[0] + FAR2[1]
 )
-SLOT = {(a % 8, b % 8): slot for slot, (a, b) in enumerate(ORDER)}
+REST = sorted({folded((a, b)) for a in range(8) for b in range(8)} - {folded(o) for o in ORDER})
+SLOT = {(a % 8, b % 8): slot for slot, (a, b) in enumerate(ORDER + REST)}
+
+
+def holders(offsets):
+    chosen = {}
+    for offset in offsets:
+        ways = [folded((offset[0] - a, offset[1] - b)) for a, b in FIRST]
+        used = list(chosen.values())
+        chosen[offset] = min(ways, key=lambda way: (abs(way[0]) + abs(way[1]), used.count(way), way))
+    return chosen
+
+
+HOLDER = holders(REST)
 
 
 def slot_of(dp, dq):
@@ -90,7 +108,9 @@
     sibling = device(x, y, z, 1 - c)
     x_peers = [device((x + d) % NX, y, z, c) for d in (2, 1, 3)]
     near = [in_plane(p + 1, q), in_plane(p - 1, q), in_plane(p, q + 1), in_plane(p, q - 1)]
-    group = [in_plane(p + dp, q + dq) for dp, dq in reversed((NEAR0 + FAR0)[1:])]
+    around = {(1, 0), (-1, 0), (0, 1), (0, -1)}
+    others = sorted(({folded(o) for o in FIRST[1:]} | set(HOLDER.values())) - around, key=lambda o: -abs(o[0]) - abs(o[1]))
+    group = [in_plane(p + dp, q + dq) for dp, dq in others]
 
     loads = [
         pltpu.make_async_copy(data_hbm, data_buf, local_sem.at[0]),
@@ -120,7 +140,7 @@
         )
 
     def to_group(i, ref):
-        for dp, dq in reversed((NEAR0 + FAR0)[1:]):
+        for dp, dq in reversed(FIRST[1:]):
             far = int((dp, dq) in FAR0)
             remote(
                 ref.at[0], ref.at[slot_of(dp, dq)], one_send.at[i, far], one_recv.at[i, far], in_plane(p - dp, q - dq)
@@ -140,7 +160,10 @@
 
     def from_group(far):
         return [
-            remote(ref.at[pl.ds(0, 7 + far)], ref.at[pl.ds(0, 7 + far)], one_send.at[i, far], one_recv.at[i, far], sibling)
+            remote(
+                ref.at[pl.ds(0, (7, 5)[far])], ref.at[pl.ds(0, (7, 5)[far])],
+                one_send.at[i, far], one_recv.at[i, far], sibling,
+            )
             for i, ref in enumerate(refs)
         ]
 
@@ -154,19 +177,22 @@
         ]
 
     def send_near(far):
-        first = 16 + 24 * far
-        for k, slots in ((0, first), (1, first + 16)):
-            for copy in to_near(k, far, 8, 8 * far, slots, near[1 - k]):
+        count = (8, 5)[far]
+        for k in range(2):
+            for copy in to_near(k, far, count, 8 * far, (13, 37)[far] + k * count, near[1 - k]):
                 copy.start()
         for side, ways in enumerate((NEAR2, FAR2)[far]):
             for dp, dq in ways:
                 held = slot_of(dp, dq + 2 * side - 1)
                 for copy in to_near(2 + side, far, 1, held, slot_of(dp, dq), near[3 - side]):
                     copy.start()
-
-    def from_near(far):
-        counts = (8, 8, 4, 4)
-        return sum((to_near(k, far, count, 0, 0, sibling) for k, count in enumerate(counts)), [])
+        if far:
+            for (dp, dq), (hp, hq) in HOLDER.items():
+                for copy in to_near(4, far, 1, slot_of(dp - hp, dq - hq), slot_of(dp, dq), in_plane(p - hp, q - hq)):
+                    copy.start()
+
+    def from_near(k, far):
+        return to_near(k, far, (8, 8, 4, 4, 0)[k] if not far else (5, 5, 3, 3, len(REST))[k], 0, 0, sibling)
 
     def to_sibling(k, start, count):
         return [
@@ -177,7 +203,9 @@
             for i, ref in enumerate(refs)
         ]
 
-    passed_on = [to_sibling(0, 0, 8), to_sibling(1, 8, 8), to_sibling(2, 16, 24), to_sibling(3, 40, 24)]
+    pieces = ((37, 5), (42, 5), (47, 3), (50, 3), (53, len(REST)))
+    passed_on = [to_sibling(0, 0, 8), to_sibling(1, 8, 5), to_sibling(2, 13, 24)]
+    last_on = [to_sibling(3 + k, *piece) for k, piece in enumerate(pieces)]
     for far in range(2):
         for copy in from_group(far):
             copy.wait_recv()
@@ -213,14 +241,15 @@
     def first_units(step, _):
         @pl.when(step == 1)
         def _():
-            for copy in from_near(0):
-                copy.wait_recv()
+            for k in range(4):
+                for copy in from_near(k, 0):
+                    copy.wait_recv()
             for copy in passed_on[2]:
                 copy.start()
             for copy in passed_on[0] + passed_on[1]:
                 copy.wait_recv()
 
-        row_unit(CHIPS * step, 16)
+        row_unit(CHIPS * step, 13)
         return 0
 
     lax.fori_loop(0, 2, first_units, 0)
@@ -231,22 +260,29 @@
             for copy in passed_on[2]:
                 copy.wait_recv()
 
-        @pl.when(step == 2)
+        row_unit(13 + CHIPS * step, 24)
+        return 0
+
+    lax.fori_loop(0, 2, next_units, 0)
+
+    def last_units(step, _):
+        @pl.when(step == 0)
         def _():
-            for copy in from_near(1):
+            for k in range(5):
+                for copy in from_near(k, 1):
+                    copy.wait_recv()
+                for copy in last_on[k]:
+                    copy.start()
+
+        @pl.when(step == 1)
+        def _():
+            for copy in sum(last_on, []):
                 copy.wait_recv()
-            for copy in passed_on[3]:
-                copy.start()
-
-        @pl.when(step == 3)
-        def _():
-            for copy in passed_on[3]:
-                copy.wait_recv()
-
-        row_unit(16 + 24 * (step // 2) + CHIPS * (step % 2), 24)
+
+        row_unit(37 + CHIPS * step, 27)
         return 0
 
-    lax.fori_loop(0, 4, next_units, 0)
+    lax.fori_loop(0, 2, last_units, 0)
 
     m = row_m[...]
     top = jnp.max(m, axis=0, keepdims=True)
@@ -347,9 +383,9 @@
     for copy in [gather_x, gather_l, gather_c, swap]:
         copy.wait_send()
     for far in range(2):
-        for copy in from_group(far) + from_near(far):
+        for copy in from_group(far) + sum((from_near(k, far) for k in range(4 + far)), []):
             copy.wait_send()
-    for copy in sum(passed_on, []):
+    for copy in sum(passed_on + last_on, []):
         copy.wait_send()
 
 
@@ -380,7 +416,7 @@
             pltpu.VMEM((2 * CHIPS, 1, 128), F32),
             pltpu.VMEM((2, 1, 128), F32),
             dma((3,)), dma, dma,
-            dma((2, 2)), dma((2, 2)), dma((2, 4, 2)), dma((2, 4, 2)), dma((2, 4)), dma((2, 4)),
+            dma((2, 2)), dma((2, 2)), dma((2, 5, 2)), dma((2, 5, 2)), dma((2, 8)), dma((2, 8)),
             dma, dma, dma, dma, dma, dma,
         ],
         compiler_params=pltpu.CompilerParams(

time: 49.7 us -> 49 us (0.986)
  Pallas kernels: 47.8 us -> 47.1 us
    pallas_call x1, Pallas kernels: 47.8 us -> 47.1 us  [per_device(): pl.pallas_call(kernel, out_shape=(jax.ShapeDtypeStruct((1, ROWS), F32), j...]
where the time goes in v6:
time: 49 us; the launch traced here: 48.8 us
  Pallas kernels  47.1 us (96%)
  local copies, waits for them, and re-layouts  1.08 us (2%)
  between operations  0.64 us (1%)
    pallas_call x1, Pallas kernels, per_device(): pl.pallas_call(kernel, out_shape=(jax.ShapeDtypeStruct((1, ROWS), F32), j...  47.1 us
    unnamed x2, local copies, waits for them, and re-layouts  1.08 us

profile of v6, /device:TPU:1, one launch (start us, length us, event | category | flops | bytes accessed | tf_op | source)
XLA Modules:
  0.0 48.8 jit_solution(14636075612388701610)
XLA Ops:
  0.6 47.1 %shard_map.50 = (f32[1,256]{1,0:T(1,128)S(1)}, f32[1,24]{1,0:T(1,128)S(1)}) custom-call(bf16[256,256]{1,0:T(8,128)(2,1)} %gen_hbm.1, bf16[24,256]{1,0:T(8,128)(2,1)} %data_hbm.1, f32[1,24]{1,0:T(1,128)} %bitcast.5), custom_call_target="tpu_custom_call" | custom-call | tf_op jit(solution)/shard_map/pallas_call | solution.py:396
  47.7 0.6 %copy.7 = f32[256]{0:T(256)} copy(f32[256]{0:T(256)S(1)} %bitcast.3) | data formatting | bytes 2048
  48.3 0.5 %copy.8 = f32[24]{0:T(128)} copy(f32[24]{0:T(128)S(1)} %bitcast.4) | data formatting | bytes 192

commit v7 on v6

--- a/solution.py
+++ b/solution.py
@@ -86,7 +86,7 @@
 
 def kernel(
     gen_hbm, data_hbm, pot_hbm, f_out, g_out,
-    x_buf, data_buf, pot_buf, sq_buf, blocks, terms, stash, row_m, row_s, row_l, send_l,
+    x_buf, gen_buf, data_buf, pot_buf, sq_buf, blocks, terms, stash, row_m, row_s, row_l,
     line_a, line_b, send_c, recv_c, final,
     local_sem, x_send, x_recv, one_send, one_recv, two_send, two_recv, sib_send, sib_recv,
     row_send, row_recv, col_send, col_recv, fin_send, fin_recv,
@@ -106,7 +106,7 @@
         return device(x, p_ + c * (q_ - p_), q_ + c * (p_ - q_), c)
 
     sibling = device(x, y, z, 1 - c)
-    x_peers = [device((x + d) % NX, y, z, c) for d in (2, 1, 3)]
+    x_peers = {d: device((x + d) % NX, y, z, c) for d in (1, 3, 2)}
     near = [in_plane(p + 1, q), in_plane(p - 1, q), in_plane(p, q + 1), in_plane(p, q - 1)]
     around = {(1, 0), (-1, 0), (0, 1), (0, -1)}
     others = sorted(({folded(o) for o in FIRST[1:]} | set(HOLDER.values())) - around, key=lambda o: -abs(o[0]) - abs(o[1]))
@@ -115,12 +115,12 @@
     loads = [
         pltpu.make_async_copy(data_hbm, data_buf, local_sem.at[0]),
         pltpu.make_async_copy(pot_hbm, pot_buf, local_sem.at[1]),
-        pltpu.make_async_copy(gen_hbm, x_buf.at[x], local_sem.at[2]),
+        pltpu.make_async_copy(gen_hbm, gen_buf, local_sem.at[2]),
     ]
     for copy in loads:
         copy.start()
 
-    peers = group + near + x_peers + [sibling]
+    peers = group + near + list(x_peers.values()) + [sibling]
     barrier = pltpu.get_barrier_semaphore()
     for peer in peers:
         pl.semaphore_signal(barrier, inc=1, device_id=peer, device_id_type=MESH)
@@ -132,6 +132,11 @@
     term = (pot_buf[...] - squares(data_buf[...])[0:1, :] * KEEP) * SCALE
     terms[0] = jnp.concatenate([term, jnp.zeros((1, 128 - COLS), F32)], axis=1)
 
+    loads[2].wait()
+    columns = jnp.transpose(gen_buf[...].astype(F32))
+    sq_buf[...] = jnp.sum(columns * columns, axis=0, keepdims=True)
+    x_buf[0] = columns.astype(BF16)
+
     pl.semaphore_wait(barrier, len(peers))
 
     def remote(src, dst, send, recv, peer):
@@ -147,14 +152,12 @@
             ).start()
 
     to_group(0, blocks)
-    for peer in x_peers:
-        remote(gen_hbm, x_buf.at[x], x_send, x_recv, peer).start()
+    for d, peer in x_peers.items():
+        remote(x_buf.at[0], x_buf.at[NX - d], x_send.at[int(d == 2)], x_recv.at[int(d == 2)], peer).start()
     to_group(1, terms)
 
     row_m[...] = jnp.full(row_m.shape, LOW, F32)
     row_s[...] = jnp.zeros(row_s.shape, F32)
-    loads[2].wait()
-    sq_buf[...] = squares(x_buf[x])[0:1, :]
 
     refs = (blocks, terms)
 
@@ -213,10 +216,13 @@
         for copy in passed_on[far]:
             copy.start()
 
-    gather_x = remote(x_buf.at[pl.ds(0, 3)], x_buf.at[pl.ds(0, 3)], x_send, x_recv, sibling)
-    gather_x.wait_recv()
-
-    def row_unit(start, count):
+    gather_x = [
+        remote(x_buf.at[pl.ds(0, n)], x_buf.at[pl.ds(0, n)], x_send.at[i], x_recv.at[i], sibling)
+        for i, n in enumerate((2, 1))
+    ]
+    gather_x[0].wait_recv()
+
+    def row_unit(start, count, which=(0, 1, 2, 3)):
         wide = blocks[pl.ds(start, count)].astype(F32)
         first = wide[:, :COLS, :].reshape(count * COLS, HALF)
         second = wide[:, COLS:, :].reshape(count * COLS, HALF)
@@ -225,9 +231,9 @@
         on_diagonal = lax.broadcasted_iota(jnp.int32, shape, 2) == lax.broadcasted_iota(jnp.int32, shape, 1)
         spread = jnp.where(on_diagonal, jnp.broadcast_to(terms[pl.ds(start, count)], shape), 0.0)
         term_ = jnp.sum(spread, axis=2, keepdims=True).reshape(count * COLS, 1)
-        for b in range(NX):
+        for b in which:
             lanes = slice(b * ROWS, (b + 1) * ROWS)
-            cross = lax.dot_general(cols, x_buf[b], (((1,), (1,)), ((), ())), preferred_element_type=F32)
+            cross = jnp.dot(cols, x_buf[b], preferred_element_type=F32)
             scores = cross * (2.0 * KEEP * SCALE) + term_
             stash[pl.ds(start, count), :, lanes] = scores.reshape(count, COLS, ROWS)
             parts = scores.reshape(count * COLS // 8, 8, ROWS)
@@ -249,10 +255,16 @@
             for copy in passed_on[0] + passed_on[1]:
                 copy.wait_recv()
 
-        row_unit(CHIPS * step, 13)
+        row_unit(CHIPS * step, 13, (0, 1, 3))
         return 0
 
+    def first_opposite(step, _):
+        row_unit(CHIPS * step, 13, (2,))
+        return 0
+
     lax.fori_loop(0, 2, first_units, 0)
+    gather_x[1].wait_recv()
+    lax.fori_loop(0, 2, first_opposite, 0)
 
     def next_units(step, _):
         @pl.when(step == 1)
@@ -284,28 +296,32 @@
 
     lax.fori_loop(0, 2, last_units, 0)
 
+    def combined(values):
+        top = jnp.max(values, axis=0)
+        return top + jnp.log2(jnp.sum(jnp.exp2(values - top[None]), axis=0))
+
     m = row_m[...]
     top = jnp.max(m, axis=0, keepdims=True)
     total = jnp.sum(row_s[...] * jnp.exp2(m - top), axis=0, keepdims=True)
-    row_l[x] = top + jnp.log2(total)
-    for peer in x_peers:
-        remote(row_l.at[x], row_l.at[x], row_send, row_recv, peer).start()
+    local = top + jnp.log2(total)
+    for b in range(NX):
+        row_l[0, b] = local[:, b * ROWS : (b + 1) * ROWS]
+    for d, peer in x_peers.items():
+        for b in range(NX):
+            remote(row_l.at[0, b], row_l.at[NX - d, (b - d) % NX], row_send, row_recv, peer).start()
     gather_l = remote(row_l.at[pl.ds(0, 3)], row_l.at[pl.ds(0, 3)], row_send, row_recv, sibling)
     gather_l.wait_recv()
-    parts = [row_l[b] for b in range(NX)]
-    top = jnp.maximum(jnp.maximum(parts[0], parts[1]), jnp.maximum(parts[2], parts[3]))
-    total = sum(jnp.exp2(part - top) for part in parts)
-    whole = top + jnp.log2(total)
-    for b in range(NX):
-        send_l[b] = whole[:, b * ROWS : (b + 1) * ROWS]
-    lifted = jnp.broadcast_to(whole, (8, NX * ROWS))
+    whole = combined(row_l[...])
+    lifted = jnp.concatenate([jnp.broadcast_to(whole[b], (8, ROWS)) for b in range(NX)], axis=1)
+
+    lane_tiles = NX * ROWS // 128
 
     def line_parts(dq, line_ref):
         for h in range(2):
             for j in range(8):
                 at = slot_of(j, dq) if h == 0 else CHIPS + slot_of(dq, j)
                 scores = stash[at].reshape(COLS // 8, 8, NX * ROWS) - lifted[None]
-                pieces = [scores[:, :, i * 128 : (i + 1) * 128] for i in range(NX * ROWS // 128)]
+                pieces = [scores[:, :, i * 128 : (i + 1) * 128] for i in range(lane_tiles)]
                 peak = pieces[0]
                 for piece in pieces[1:]:
                     peak = jnp.maximum(peak, piece)
@@ -314,10 +330,6 @@
                     added = added + jnp.exp2(piece - peak)
                 to = (2 * j + h) * COLS
                 line_ref[to : to + COLS, :] = (peak + jnp.log2(added)).reshape(COLS, 128)
-
-    def combined(values):
-        top = jnp.max(values, axis=0)
-        return top + jnp.log2(jnp.sum(jnp.exp2(values - top[None]), axis=0))
 
     def tiles_of(j):
         first = 2 * COLS * j // 128
@@ -347,7 +359,7 @@
             line_parts(FAR_FIRST[i + 1], room[(i + 1) % 2])
         line_send(FAR_FIRST[i], room[i % 2])
 
-    f_out[...] = sq_buf[...] * KEEP - (EPS * LN2) * send_l[x] + EPS * math.log(float(CHIPS * NX * NC * COLS))
+    f_out[...] = sq_buf[...] * KEEP - (EPS * LN2) * whole[0] + EPS * math.log(float(CHIPS * NX * NC * COLS))
 
     tiles = 8 * sum(tiles_of(j)[1] for j in range(8)) - 1
     gather_c = remote(recv_c.at[pl.ds(0, tiles)], recv_c.at[pl.ds(0, tiles)], col_send, col_recv, sibling)
@@ -380,7 +392,7 @@
         math.log(float(CHIPS * NX * NC * ROWS)) - math.log(float(CHIPS * NX * NC * COLS))
     )
 
-    for copy in [gather_x, gather_l, gather_c, swap]:
+    for copy in gather_x + [gather_l, gather_c, swap]:
         copy.wait_send()
     for far in range(2):
         for copy in from_group(far) + sum((from_near(k, far) for k in range(4 + far)), []):
@@ -399,7 +411,8 @@
         in_specs=[hbm, hbm, hbm],
         out_specs=(vmem, vmem),
         scratch_shapes=[
-            pltpu.VMEM((NX, ROWS, WIDTH), BF16),
+            pltpu.VMEM((NX, WIDTH, ROWS), BF16),
+            pltpu.VMEM((ROWS, WIDTH), BF16),
             pltpu.VMEM((COLS, WIDTH), BF16),
             pltpu.VMEM((1, COLS), F32),
             pltpu.VMEM((1, ROWS), F32),
@@ -408,14 +421,13 @@
             pltpu.VMEM((2 * CHIPS, COLS, NX * ROWS), F32),
             pltpu.VMEM((8, NX * ROWS), F32),
             pltpu.VMEM((8, NX * ROWS), F32),
-            pltpu.VMEM((NX, 1, NX * ROWS), F32),
-            pltpu.VMEM((NX, 1, ROWS), F32),
+            pltpu.VMEM((NX, NX, 1, ROWS), F32),
             pltpu.VMEM((LINE, 128), F32),
             pltpu.VMEM((LINE, 128), F32),
             pltpu.VMEM((8, LINE // 128, 1, 128), F32),
             pltpu.VMEM((2 * CHIPS, 1, 128), F32),
             pltpu.VMEM((2, 1, 128), F32),
-            dma((3,)), dma, dma,
+            dma((3,)), dma((2,)), dma((2,)),
             dma((2, 2)), dma((2, 2)), dma((2, 5, 2)), dma((2, 5, 2)), dma((2, 8)), dma((2, 8)),
             dma, dma, dma, dma, dma, dma,
         ],

time: 49 us -> 49 us (level)
  no operation moved by 1% of the time
where the time goes in v7:
time: 49 us; the launch traced here: 48.9 us
  Pallas kernels  47.1 us (96%)
  local copies, waits for them, and re-layouts  1.08 us (2%)
  between operations  0.64 us (1%)
    pallas_call x1, Pallas kernels, per_device(): pl.pallas_call(kernel, out_shape=(jax.ShapeDtypeStruct((1, ROWS), F32), j...  47.1 us
    unnamed x2, local copies, waits for them, and re-layouts  1.08 us

profile of v7, /device:TPU:1, one launch (start us, length us, event | category | flops | bytes accessed | tf_op | source)
XLA Modules:
  0.0 48.9 jit_solution(5090352872591959909)
XLA Ops:
  0.6 47.1 %shard_map.50 = (f32[1,256]{1,0:T(1,128)S(1)}, f32[1,24]{1,0:T(1,128)S(1)}) custom-call(bf16[256,256]{1,0:T(8,128)(2,1)} %gen_hbm.1, bf16[24,256]{1,0:T(8,128)(2,1)} %data_hbm.1, f32[1,24]{1,0:T(1,128)} %bitcast.5), custom_call_target="tpu_custom_call" | custom-call | tf_op jit(solution)/shard_map/pallas_call | solution.py:408
  47.8 0.6 %copy.7 = f32[256]{0:T(256)} copy(f32[256]{0:T(256)S(1)} %bitcast.3) | data formatting | bytes 2048
  48.3 0.5 %copy.8 = f32[24]{0:T(128)} copy(f32[24]{0:T(128)S(1)} %bitcast.4) | data formatting | bytes 192

commit v8 on v7

--- a/solution.py
+++ b/solution.py
@@ -21,7 +21,6 @@
 ROWS = 256
 COLS = 24
 WIDTH = 256
-HALF = WIDTH // 2
 LINE = 8 * NC * COLS
 KEEP = 1.0 / WIDTH
 
@@ -86,7 +85,7 @@
 
 def kernel(
     gen_hbm, data_hbm, pot_hbm, f_out, g_out,
-    x_buf, gen_buf, data_buf, pot_buf, sq_buf, blocks, terms, stash, row_m, row_s, row_l,
+    x_buf, pot_buf, sq_buf, blocks, terms, stash, row_m, row_s, row_l,
     line_a, line_b, send_c, recv_c, final,
     local_sem, x_send, x_recv, one_send, one_recv, two_send, two_recv, sib_send, sib_recv,
     row_send, row_recv, col_send, col_recv, fin_send, fin_recv,
@@ -113,9 +112,9 @@
     group = [in_plane(p + dp, q + dq) for dp, dq in others]
 
     loads = [
-        pltpu.make_async_copy(data_hbm, data_buf, local_sem.at[0]),
+        pltpu.make_async_copy(data_hbm, blocks.at[0], local_sem.at[0]),
         pltpu.make_async_copy(pot_hbm, pot_buf, local_sem.at[1]),
-        pltpu.make_async_copy(gen_hbm, gen_buf, local_sem.at[2]),
+        pltpu.make_async_copy(gen_hbm, x_buf.at[0], local_sem.at[2]),
     ]
     for copy in loads:
         copy.start()
@@ -125,18 +124,6 @@
     for peer in peers:
         pl.semaphore_signal(barrier, inc=1, device_id=peer, device_id_type=MESH)
 
-    for copy in loads[:2]:
-        copy.wait()
-    data = data_buf[...].astype(F32)
-    blocks[0] = jnp.concatenate([data[:, :HALF], data[:, HALF:]], axis=0).astype(BF16)
-    term = (pot_buf[...] - squares(data_buf[...])[0:1, :] * KEEP) * SCALE
-    terms[0] = jnp.concatenate([term, jnp.zeros((1, 128 - COLS), F32)], axis=1)
-
-    loads[2].wait()
-    columns = jnp.transpose(gen_buf[...].astype(F32))
-    sq_buf[...] = jnp.sum(columns * columns, axis=0, keepdims=True)
-    x_buf[0] = columns.astype(BF16)
-
     pl.semaphore_wait(barrier, len(peers))
 
     def remote(src, dst, send, recv, peer):
@@ -144,20 +131,27 @@
             src_ref=src, dst_ref=dst, send_sem=send, recv_sem=recv, device_id=peer, device_id_type=MESH
         )
 
-    def to_group(i, ref):
+    def to_group(i, ref, source):
         for dp, dq in reversed(FIRST[1:]):
             far = int((dp, dq) in FAR0)
             remote(
-                ref.at[0], ref.at[slot_of(dp, dq)], one_send.at[i, far], one_recv.at[i, far], in_plane(p - dp, q - dq)
+                source, ref.at[slot_of(dp, dq)], one_send.at[i, far], one_recv.at[i, far], in_plane(p - dp, q - dq)
             ).start()
 
-    to_group(0, blocks)
+    to_group(0, blocks, data_hbm)
     for d, peer in x_peers.items():
-        remote(x_buf.at[0], x_buf.at[NX - d], x_send.at[int(d == 2)], x_recv.at[int(d == 2)], peer).start()
-    to_group(1, terms)
+        remote(gen_hbm, x_buf.at[NX - d], x_send.at[int(d == 2)], x_recv.at[int(d == 2)], peer).start()
+
+    for copy in loads[:2]:
+        copy.wait()
+    term = (pot_buf[...] - squares(blocks[0])[0:1, :] * KEEP) * SCALE
+    terms[0] = jnp.concatenate([term, jnp.zeros((1, 128 - COLS), F32)], axis=1)
+    to_group(1, terms, terms.at[0])
 
     row_m[...] = jnp.full(row_m.shape, LOW, F32)
     row_s[...] = jnp.zeros(row_s.shape, F32)
+    loads[2].wait()
+    sq_buf[...] = squares(x_buf[0])[0:1, :]
 
     refs = (blocks, terms)
 
@@ -179,20 +173,17 @@
             for i, ref in enumerate(refs)
         ]
 
-    def send_near(far):
+    def send_near(i, far):
         count = (8, 5)[far]
         for k in range(2):
-            for copy in to_near(k, far, count, 8 * far, (13, 37)[far] + k * count, near[1 - k]):
-                copy.start()
+            to_near(k, far, count, 8 * far, (13, 37)[far] + k * count, near[1 - k])[i].start()
         for side, ways in enumerate((NEAR2, FAR2)[far]):
             for dp, dq in ways:
                 held = slot_of(dp, dq + 2 * side - 1)
-                for copy in to_near(2 + side, far, 1, held, slot_of(dp, dq), near[3 - side]):
-                    copy.start()
+                to_near(2 + side, far, 1, held, slot_of(dp, dq), near[3 - side])[i].start()
         if far:
             for (dp, dq), (hp, hq) in HOLDER.items():
-                for copy in to_near(4, far, 1, slot_of(dp - hp, dq - hq), slot_of(dp, dq), in_plane(p - hp, q - hq)):
-                    copy.start()
+                to_near(4, far, 1, slot_of(dp - hp, dq - hq), slot_of(dp, dq), in_plane(p - hp, q - hq))[i].start()
 
     def from_near(k, far):
         return to_near(k, far, (8, 8, 4, 4, 0)[k] if not far else (5, 5, 3, 3, len(REST))[k], 0, 0, sibling)
@@ -210,11 +201,10 @@
     passed_on = [to_sibling(0, 0, 8), to_sibling(1, 8, 5), to_sibling(2, 13, 24)]
     last_on = [to_sibling(3 + k, *piece) for k, piece in enumerate(pieces)]
     for far in range(2):
-        for copy in from_group(far):
-            copy.wait_recv()
-        send_near(far)
-        for copy in passed_on[far]:
-            copy.start()
+        for i in range(2):
+            from_group(far)[i].wait_recv()
+            send_near(i, far)
+            passed_on[far][i].start()
 
     gather_x = [
         remote(x_buf.at[pl.ds(0, n)], x_buf.at[pl.ds(0, n)], x_send.at[i], x_recv.at[i], sibling)
@@ -223,17 +213,14 @@
     gather_x[0].wait_recv()
 
     def row_unit(start, count, which=(0, 1, 2, 3)):
-        wide = blocks[pl.ds(start, count)].astype(F32)
-        first = wide[:, :COLS, :].reshape(count * COLS, HALF)
-        second = wide[:, COLS:, :].reshape(count * COLS, HALF)
-        cols = jnp.concatenate([first.astype(BF16), second.astype(BF16)], axis=1)
+        cols = blocks[pl.ds(start, count)].astype(F32).reshape(count * COLS, WIDTH).astype(BF16)
         shape = (count, COLS, 128)
         on_diagonal = lax.broadcasted_iota(jnp.int32, shape, 2) == lax.broadcasted_iota(jnp.int32, shape, 1)
         spread = jnp.where(on_diagonal, jnp.broadcast_to(terms[pl.ds(start, count)], shape), 0.0)
         term_ = jnp.sum(spread, axis=2, keepdims=True).reshape(count * COLS, 1)
         for b in which:
             lanes = slice(b * ROWS, (b + 1) * ROWS)
-            cross = jnp.dot(cols, x_buf[b], preferred_element_type=F32)
+            cross = lax.dot_general(cols, x_buf[b], (((1,), (1,)), ((), ())), preferred_element_type=F32)
             scores = cross * (2.0 * KEEP * SCALE) + term_
             stash[pl.ds(start, count), :, lanes] = scores.reshape(count, COLS, ROWS)
             parts = scores.reshape(count * COLS // 8, 8, ROWS)
@@ -411,12 +398,10 @@
         in_specs=[hbm, hbm, hbm],
         out_specs=(vmem, vmem),
         scratch_shapes=[
-            pltpu.VMEM((NX, WIDTH, ROWS), BF16),
-            pltpu.VMEM((ROWS, WIDTH), BF16),
-            pltpu.VMEM((COLS, WIDTH), BF16),
+            pltpu.VMEM((NX, ROWS, WIDTH), BF16),
             pltpu.VMEM((1, COLS), F32),
             pltpu.VMEM((1, ROWS), F32),
-            pltpu.VMEM((2 * CHIPS, 2 * COLS, HALF), BF16),
+            pltpu.VMEM((2 * CHIPS, COLS, WIDTH), BF16),
             pltpu.VMEM((2 * CHIPS, 1, 128), F32),
             pltpu.VMEM((2 * CHIPS, COLS, NX * ROWS), F32),
             pltpu.VMEM((8, NX * ROWS), F32),

time: 49 us -> 48.3 us (0.986)
  Pallas kernels: 47.1 us -> 46.5 us
    pallas_call x1, Pallas kernels: 47.1 us -> 46.5 us  [per_device(): pl.pallas_call(kernel, out_shape=(jax.ShapeDtypeStruct((1, ROWS), F32), j...]
where the time goes in v8:
time: 48.3 us; the launch traced here: 48.2 us
  Pallas kernels  46.5 us (96%)
  local copies, waits for them, and re-layouts  1.08 us (2%)
  between operations  0.64 us (1%)
    pallas_call x1, Pallas kernels, per_device(): pl.pallas_call(kernel, out_shape=(jax.ShapeDtypeStruct((1, ROWS), F32), j...  46.5 us
    unnamed x2, local copies, waits for them, and re-layouts  1.08 us

profile of v8, /device:TPU:1, one launch (start us, length us, event | category | flops | bytes accessed | tf_op | source)
XLA Modules:
  0.0 48.2 jit_solution(7823813425881927938)
XLA Ops:
  0.6 46.5 %shard_map.50 = (f32[1,256]{1,0:T(1,128)S(1)}, f32[1,24]{1,0:T(1,128)S(1)}) custom-call(bf16[256,256]{1,0:T(8,128)(2,1)} %gen_hbm.1, bf16[24,256]{1,0:T(8,128)(2,1)} %data_hbm.1, f32[1,24]{1,0:T(1,128)} %bitcast.5), custom_call_target="tpu_custom_call" | custom-call | tf_op jit(solution)/shard_map/pallas_call | solution.py:395
  47.1 0.6 %copy.7 = f32[256]{0:T(256)} copy(f32[256]{0:T(256)S(1)} %bitcast.3) | data formatting | bytes 2048
  47.7 0.5 %copy.8 = f32[24]{0:T(128)} copy(f32[24]{0:T(128)S(1)} %bitcast.4) | data formatting | bytes 192

commit v9 on v8

--- a/solution.py
+++ b/solution.py
@@ -21,15 +21,13 @@
 ROWS = 256
 COLS = 24
 WIDTH = 256
-LINE = 8 * NC * COLS
+BATCH = 8 * NC * COLS
 KEEP = 1.0 / WIDTH
 
 
 def hops(d):
     return min(d % 8, -d % 8)
 
-
-FAR_FIRST = (4, 3, 5, 2, 6, 1, 7, 0)
 
 NEAR0 = [(0, 0), (0, 2), (0, -2), (2, 1), (2, -1), (-2, 1), (-2, -1), (0, 4)]
 FAR0 = [(4, 0), (2, 3), (2, -3), (-2, 3), (-2, -3)]
@@ -65,6 +63,8 @@
 
 
 HOLDER = holders(REST)
+ALL = sorted((folded((a, b)) for a in range(8) for b in range(8)), key=lambda o: (-abs(o[0]) - abs(o[1]), o))
+BATCHES = [ALL[i : i + 8] for i in range(0, 56, 8)] + [ALL[:55:-1]]
 
 
 def slot_of(dp, dq):
@@ -86,7 +86,7 @@
 def kernel(
     gen_hbm, data_hbm, pot_hbm, f_out, g_out,
     x_buf, pot_buf, sq_buf, blocks, terms, stash, row_m, row_s, row_l,
-    line_a, line_b, send_c, recv_c, final,
+    batch_a, batch_b, send_c, recv_c, final,
     local_sem, x_send, x_recv, one_send, one_recv, two_send, two_recv, sib_send, sib_recv,
     row_send, row_recv, col_send, col_recv, fin_send, fin_recv,
 ):
@@ -303,10 +303,9 @@
 
     lane_tiles = NX * ROWS // 128
 
-    def line_parts(dq, line_ref):
-        for h in range(2):
-            for j in range(8):
-                at = slot_of(j, dq) if h == 0 else CHIPS + slot_of(dq, j)
+    def batch_parts(batch, batch_ref):
+        for j, (dp, dq) in enumerate(batch):
+            for h, at in enumerate((slot_of(dp, dq), CHIPS + slot_of(dq, dp))):
                 scores = stash[at].reshape(COLS // 8, 8, NX * ROWS) - lifted[None]
                 pieces = [scores[:, :, i * 128 : (i + 1) * 128] for i in range(lane_tiles)]
                 peak = pieces[0]
@@ -316,48 +315,54 @@
                 for piece in pieces[1:]:
                     added = added + jnp.exp2(piece - peak)
                 to = (2 * j + h) * COLS
-                line_ref[to : to + COLS, :] = (peak + jnp.log2(added)).reshape(COLS, 128)
+                batch_ref[to : to + COLS, :] = (peak + jnp.log2(added)).reshape(COLS, 128)
 
     def tiles_of(j):
         first = 2 * COLS * j // 128
         return first, (2 * COLS * (j + 1) - 1) // 128 - first + 1
 
-    def line_send(dq, line_ref):
-        values = jnp.transpose(line_ref[...])
+    def batch_send(i, batch_ref):
+        values = jnp.transpose(batch_ref[...])
         top = jnp.max(values, axis=0, keepdims=True)
         sums = top + jnp.log2(jnp.sum(jnp.exp2(values - top), axis=0, keepdims=True))
-        for t in range(LINE // 128):
-            send_c[dq, t] = sums[:, 128 * t : 128 * (t + 1)]
-        for dp in FAR_FIRST:
-            first, count = tiles_of(dp)
+        for t in range(BATCH // 128):
+            send_c[i, t] = sums[:, 128 * t : 128 * (t + 1)]
+        for j, (dp, dq) in enumerate(BATCHES[i]):
+            first, count = tiles_of(j)
+            seen = 2 * (8 * j + i)
             if (dp, dq) == (0, 0):
-                recv_c[0] = sums[:, :128]
+                recv_c[seen] = sums[:, :128]
             else:
-                seen = 2 * ((-dp % 8) * 8 + -dq % 8)
                 remote(
-                    send_c.at[dq, pl.ds(first, count)], recv_c.at[pl.ds(seen, count)],
+                    send_c.at[i, pl.ds(first, count)], recv_c.at[pl.ds(seen, count)],
                     col_send, col_recv, in_plane(p + dp, q + dq),
                 ).start()
 
-    room = (line_a, line_b)
-    line_parts(FAR_FIRST[0], room[0])
+    room = (batch_a, batch_b)
+    batch_parts(BATCHES[0], room[0])
     for i in range(8):
         if i < 7:
-            line_parts(FAR_FIRST[i + 1], room[(i + 1) % 2])
-        line_send(FAR_FIRST[i], room[i % 2])
+            batch_parts(BATCHES[i + 1], room[(i + 1) % 2])
+        batch_send(i, room[i % 2])
 
     f_out[...] = sq_buf[...] * KEEP - (EPS * LN2) * whole[0] + EPS * math.log(float(CHIPS * NX * NC * COLS))
 
     tiles = 8 * sum(tiles_of(j)[1] for j in range(8)) - 1
     gather_c = remote(recv_c.at[pl.ds(0, tiles)], recv_c.at[pl.ds(0, tiles)], col_send, col_recv, sibling)
+    for copy in gather_x + [gather_l]:
+        copy.wait_send()
+    for far in range(2):
+        for copy in from_group(far) + sum((from_near(k, far) for k in range(4 + far)), []):
+            copy.wait_send()
+    for copy in sum(passed_on + last_on, []):
+        copy.wait_send()
     gather_c.wait_recv()
 
     parts = []
-    for dp in range(8):
-        j = -dp % 8
+    for j in range(8):
         first, count = tiles_of(j)
         tiles = [
-            combined(jnp.concatenate([recv_c[pl.ds(2 * (8 * dp + dq) + t, 1)] for dq in range(8)], axis=0))
+            combined(jnp.concatenate([recv_c[pl.ds(2 * (8 * j + i) + t, 1)] for i in range(8)], axis=0))
             for t in range(count)
         ]
         row = jnp.concatenate(tiles, axis=1)
@@ -379,13 +384,8 @@
         math.log(float(CHIPS * NX * NC * ROWS)) - math.log(float(CHIPS * NX * NC * COLS))
     )
 
-    for copy in gather_x + [gather_l, gather_c, swap]:
-        copy.wait_send()
-    for far in range(2):
-        for copy in from_group(far) + sum((from_near(k, far) for k in range(4 + far)), []):
-            copy.wait_send()
-    for copy in sum(passed_on + last_on, []):
-        copy.wait_send()
+    gather_c.wait_send()
+    swap.wait_send()
 
 
 def per_device(gen_samples, data_samples, data_potential):
@@ -407,9 +407,9 @@
             pltpu.VMEM((8, NX * ROWS), F32),
             pltpu.VMEM((8, NX * ROWS), F32),
             pltpu.VMEM((NX, NX, 1, ROWS), F32),
-            pltpu.VMEM((LINE, 128), F32),
-            pltpu.VMEM((LINE, 128), F32),
-            pltpu.VMEM((8, LINE // 128, 1, 128), F32),
+            pltpu.VMEM((BATCH, 128), F32),
+            pltpu.VMEM((BATCH, 128), F32),
+            pltpu.VMEM((8, BATCH // 128, 1, 128), F32),
             pltpu.VMEM((2 * CHIPS, 1, 128), F32),
             pltpu.VMEM((2, 1, 128), F32),
             dma((3,)), dma((2,)), dma((2,)),

time: 48.3 us -> 47.6 us (0.986)
  Pallas kernels: 46.5 us -> 45.8 us
    pallas_call x1, Pallas kernels: 46.5 us -> 45.8 us  [per_device(): pl.pallas_call(kernel, out_shape=(jax.ShapeDtypeStruct((1, ROWS), F32), j...]
where the time goes in v9:
time: 47.6 us; the launch traced here: 47.5 us
  Pallas kernels  45.8 us (96%)
  local copies, waits for them, and re-layouts  1.08 us (2%)
  between operations  0.64 us (1%)
    pallas_call x1, Pallas kernels, per_device(): pl.pallas_call(kernel, out_shape=(jax.ShapeDtypeStruct((1, ROWS), F32), j...  45.8 us
    unnamed x2, local copies, waits for them, and re-layouts  1.08 us

profile of v9, /device:TPU:1, one launch (start us, length us, event | category | flops | bytes accessed | tf_op | source)
XLA Modules:
  0.0 47.5 jit_solution(14905157446397197187)
XLA Ops:
  0.6 45.8 %shard_map.50 = (f32[1,256]{1,0:T(1,128)S(1)}, f32[1,24]{1,0:T(1,128)S(1)}) custom-call(bf16[256,256]{1,0:T(8,128)(2,1)} %gen_hbm.1, bf16[24,256]{1,0:T(8,128)(2,1)} %data_hbm.1, f32[1,24]{1,0:T(1,128)} %bitcast.5), custom_call_target="tpu_custom_call" | custom-call | tf_op jit(solution)/shard_map/pallas_call | solution.py:395
  46.4 0.6 %copy.7 = f32[256]{0:T(256)} copy(f32[256]{0:T(256)S(1)} %bitcast.3) | data formatting | bytes 2048
  47.0 0.5 %copy.8 = f32[24]{0:T(128)} copy(f32[24]{0:T(128)S(1)} %bitcast.4) | data formatting | bytes 192

commit v10 on v9

--- a/solution.py
+++ b/solution.py
@@ -44,13 +44,9 @@
 
 
 FIRST = NEAR0 + FAR0
-ORDER = (
-    FIRST
-    + shifted(NEAR0, 1, 0) + shifted(NEAR0, -1, 0) + NEAR2[0] + NEAR2[1]
-    + shifted(FAR0, 1, 0) + shifted(FAR0, -1, 0) + FAR2[0] + FAR2[1]
-)
-REST = sorted({folded((a, b)) for a in range(8) for b in range(8)} - {folded(o) for o in ORDER})
-SLOT = {(a % 8, b % 8): slot for slot, (a, b) in enumerate(ORDER + REST)}
+NEAR = shifted(NEAR0, 1, 0) + shifted(NEAR0, -1, 0) + NEAR2[0] + NEAR2[1]
+FAR = shifted(FAR0, 1, 0) + shifted(FAR0, -1, 0) + FAR2[0] + FAR2[1]
+REST = sorted({folded((a, b)) for a in range(8) for b in range(8)} - {folded(o) for o in FIRST + NEAR + FAR})
 
 
 def holders(offsets):
@@ -63,6 +59,17 @@
 
 
 HOLDER = holders(REST)
+NEAR0_SET = {folded(o) for o in NEAR0}
+REST_PARTS = ([], [])
+for rest in REST:
+    held = folded((rest[0] - HOLDER[rest][0], rest[1] - HOLDER[rest][1]))
+    REST_PARTS[held not in NEAR0_SET].append(rest)
+ORDER = FIRST + NEAR + REST_PARTS[0] + FAR + REST_PARTS[1]
+SLOT = {(a % 8, b % 8): slot for slot, (a, b) in enumerate(ORDER)}
+FIRST_NEAR, FIRST_FAR = len(FIRST), len(FIRST + NEAR + REST_PARTS[0])
+COUNTS = ((8, 8, 4, 4, len(REST_PARTS[0])), (5, 5, 3, 3, len(REST_PARTS[1])))
+
+
 ALL = sorted((folded((a, b)) for a in range(8) for b in range(8)), key=lambda o: (-abs(o[0]) - abs(o[1]), o))
 BATCHES = [ALL[i : i + 8] for i in range(0, 56, 8)] + [ALL[:55:-1]]
 
@@ -174,19 +181,19 @@
         ]
 
     def send_near(i, far):
-        count = (8, 5)[far]
+        count = COUNTS[far][0]
+        for dp, dq in REST_PARTS[far]:
+            hp, hq = HOLDER[dp, dq]
+            to_near(4, far, 1, slot_of(dp - hp, dq - hq), slot_of(dp, dq), in_plane(p - hp, q - hq))[i].start()
         for k in range(2):
-            to_near(k, far, count, 8 * far, (13, 37)[far] + k * count, near[1 - k])[i].start()
+            to_near(k, far, count, 8 * far, (FIRST_NEAR, FIRST_FAR)[far] + k * count, near[1 - k])[i].start()
         for side, ways in enumerate((NEAR2, FAR2)[far]):
             for dp, dq in ways:
                 held = slot_of(dp, dq + 2 * side - 1)
                 to_near(2 + side, far, 1, held, slot_of(dp, dq), near[3 - side])[i].start()
-        if far:
-            for (dp, dq), (hp, hq) in HOLDER.items():
-                to_near(4, far, 1, slot_of(dp - hp, dq - hq), slot_of(dp, dq), in_plane(p - hp, q - hq))[i].start()
 
     def from_near(k, far):
-        return to_near(k, far, (8, 8, 4, 4, 0)[k] if not far else (5, 5, 3, 3, len(REST))[k], 0, 0, sibling)
+        return to_near(k, far, COUNTS[far][k], 0, 0, sibling)
 
     def to_sibling(k, start, count):
         return [
@@ -197,9 +204,8 @@
             for i, ref in enumerate(refs)
         ]
 
-    pieces = ((37, 5), (42, 5), (47, 3), (50, 3), (53, len(REST)))
-    passed_on = [to_sibling(0, 0, 8), to_sibling(1, 8, 5), to_sibling(2, 13, 24)]
-    last_on = [to_sibling(3 + k, *piece) for k, piece in enumerate(pieces)]
+    passed_on = [to_sibling(0, 0, 8), to_sibling(1, 8, 5), to_sibling(2, FIRST_NEAR, sum(COUNTS[0]))]
+    last_on = [to_sibling(3 + k, FIRST_FAR + sum(COUNTS[1][:k]), COUNTS[1][k]) for k in range(5)]
     for far in range(2):
         for i in range(2):
             from_group(far)[i].wait_recv()
@@ -234,7 +240,7 @@
     def first_units(step, _):
         @pl.when(step == 1)
         def _():
-            for k in range(4):
+            for k in range(5):
                 for copy in from_near(k, 0):
                     copy.wait_recv()
             for copy in passed_on[2]:
@@ -259,7 +265,7 @@
             for copy in passed_on[2]:
                 copy.wait_recv()
 
-        row_unit(13 + CHIPS * step, 24)
+        row_unit(FIRST_NEAR + CHIPS * step, sum(COUNTS[0]))
         return 0
 
     lax.fori_loop(0, 2, next_units, 0)
@@ -278,7 +284,7 @@
             for copy in sum(last_on, []):
                 copy.wait_recv()
 
-        row_unit(37 + CHIPS * step, 27)
+        row_unit(FIRST_FAR + CHIPS * step, sum(COUNTS[1]))
         return 0
 
     lax.fori_loop(0, 2, last_units, 0)
@@ -352,7 +358,7 @@
     for copy in gather_x + [gather_l]:
         copy.wait_send()
     for far in range(2):
-        for copy in from_group(far) + sum((from_near(k, far) for k in range(4 + far)), []):
+        for copy in from_group(far) + sum((from_near(k, far) for k in range(5)), []):
             copy.wait_send()
     for copy in sum(passed_on + last_on, []):
         copy.wait_send()

time: 47.6 us -> 48.9 us (1.027)
  Pallas kernels: 45.8 us -> 47.1 us
    pallas_call x1, Pallas kernels: 45.8 us -> 47.1 us  [per_device(): pl.pallas_call(kernel, out_shape=(jax.ShapeDtypeStruct((1, ROWS), F32), j...]
where the time goes in v10:
time: 48.9 us; the launch traced here: 48.8 us
  Pallas kernels  47.1 us (96%)
  local copies, waits for them, and re-layouts  1.08 us (2%)
  between operations  0.64 us (1%)
    pallas_call x1, Pallas kernels, per_device(): pl.pallas_call(kernel, out_shape=(jax.ShapeDtypeStruct((1, ROWS), F32), j...  47.1 us
    unnamed x2, local copies, waits for them, and re-layouts  1.08 us

profile of v10, /device:TPU:1, one launch (start us, length us, event | category | flops | bytes accessed | tf_op | source)
XLA Modules:
  0.0 48.8 jit_solution(14729081672835034558)
XLA Ops:
  0.6 47.1 %shard_map.50 = (f32[1,256]{1,0:T(1,128)S(1)}, f32[1,24]{1,0:T(1,128)S(1)}) custom-call(bf16[256,256]{1,0:T(8,128)(2,1)} %gen_hbm.1, bf16[24,256]{1,0:T(8,128)(2,1)} %data_hbm.1, f32[1,24]{1,0:T(1,128)} %bitcast.5), custom_call_target="tpu_custom_call" | custom-call | tf_op jit(solution)/shard_map/pallas_call | solution.py:401
  47.7 0.6 %copy.7 = f32[256]{0:T(256)} copy(f32[256]{0:T(256)S(1)} %bitcast.3) | data formatting | bytes 2048
  48.3 0.5 %copy.8 = f32[24]{0:T(128)} copy(f32[24]{0:T(128)S(1)} %bitcast.4) | data formatting | bytes 192

commit v11 on v9

--- a/solution.py
+++ b/solution.py
@@ -198,8 +198,9 @@
         ]
 
     pieces = ((37, 5), (42, 5), (47, 3), (50, 3), (53, len(REST)))
-    passed_on = [to_sibling(0, 0, 8), to_sibling(1, 8, 5), to_sibling(2, 13, 24)]
-    last_on = [to_sibling(3 + k, *piece) for k, piece in enumerate(pieces)]
+    passed_on = [to_sibling(0, 0, 8), to_sibling(1, 8, 5)]
+    near_on = [to_sibling(2 + k, *piece) for k, piece in enumerate(((13, 8), (21, 8), (29, 4), (33, 4)))]
+    last_on = [to_sibling(6 + k, *piece) for k, piece in enumerate(pieces)]
     for far in range(2):
         for i in range(2):
             from_group(far)[i].wait_recv()
@@ -234,29 +235,32 @@
     def first_units(step, _):
         @pl.when(step == 1)
         def _():
+            for copy in passed_on[0] + passed_on[1]:
+                copy.wait_recv()
+
+        row_unit(CHIPS * step, 13, (0, 1, 3))
+        return 0
+
+    def first_opposite(step, _):
+        row_unit(CHIPS * step, 13, (2,))
+        return 0
+
+    lax.fori_loop(0, 2, first_units, 0)
+    gather_x[1].wait_recv()
+    lax.fori_loop(0, 2, first_opposite, 0)
+
+    def next_units(step, _):
+        @pl.when(step == 0)
+        def _():
             for k in range(4):
                 for copy in from_near(k, 0):
                     copy.wait_recv()
-            for copy in passed_on[2]:
-                copy.start()
-            for copy in passed_on[0] + passed_on[1]:
-                copy.wait_recv()
-
-        row_unit(CHIPS * step, 13, (0, 1, 3))
-        return 0
-
-    def first_opposite(step, _):
-        row_unit(CHIPS * step, 13, (2,))
-        return 0
-
-    lax.fori_loop(0, 2, first_units, 0)
-    gather_x[1].wait_recv()
-    lax.fori_loop(0, 2, first_opposite, 0)
-
-    def next_units(step, _):
+                for copy in near_on[k]:
+                    copy.start()
+
         @pl.when(step == 1)
         def _():
-            for copy in passed_on[2]:
+            for copy in sum(near_on, []):
                 copy.wait_recv()
 
         row_unit(13 + CHIPS * step, 24)
@@ -354,7 +358,7 @@
     for far in range(2):
         for copy in from_group(far) + sum((from_near(k, far) for k in range(4 + far)), []):
             copy.wait_send()
-    for copy in sum(passed_on + last_on, []):
+    for copy in sum(passed_on + near_on + last_on, []):
         copy.wait_send()
     gather_c.wait_recv()
 
@@ -413,7 +417,7 @@
             pltpu.VMEM((2 * CHIPS, 1, 128), F32),
             pltpu.VMEM((2, 1, 128), F32),
             dma((3,)), dma((2,)), dma((2,)),
-            dma((2, 2)), dma((2, 2)), dma((2, 5, 2)), dma((2, 5, 2)), dma((2, 8)), dma((2, 8)),
+            dma((2, 2)), dma((2, 2)), dma((2, 5, 2)), dma((2, 5, 2)), dma((2, 11)), dma((2, 11)),
             dma, dma, dma, dma, dma, dma,
         ],
         compiler_params=pltpu.CompilerParams(

time: 47.6 us -> 47.7 us (level)
  no operation moved by 1% of the time
where the time goes in v11:
time: 47.7 us; the launch traced here: 47.6 us
  Pallas kernels  45.8 us (96%)
  local copies, waits for them, and re-layouts  1.08 us (2%)
  between operations  0.64 us (1%)
    pallas_call x1, Pallas kernels, per_device(): pl.pallas_call(kernel, out_shape=(jax.ShapeDtypeStruct((1, ROWS), F32), j...  45.8 us
    unnamed x2, local copies, waits for them, and re-layouts  1.08 us

profile of v11, /device:TPU:1, one launch (start us, length us, event | category | flops | bytes accessed | tf_op | source)
XLA Modules:
  0.0 47.6 jit_solution(5775587328526779868)
XLA Ops:
  0.6 45.8 %shard_map.50 = (f32[1,256]{1,0:T(1,128)S(1)}, f32[1,24]{1,0:T(1,128)S(1)}) custom-call(bf16[256,256]{1,0:T(8,128)(2,1)} %gen_hbm.1, bf16[24,256]{1,0:T(8,128)(2,1)} %data_hbm.1, f32[1,24]{1,0:T(1,128)} %bitcast.5), custom_call_target="tpu_custom_call" | custom-call | tf_op jit(solution)/shard_map/pallas_call | solution.py:399
  46.5 0.6 %copy.7 = f32[256]{0:T(256)} copy(f32[256]{0:T(256)S(1)} %bitcast.3) | data formatting | bytes 2048
  47.0 0.5 %copy.8 = f32[24]{0:T(128)} copy(f32[24]{0:T(128)S(1)} %bitcast.4) | data formatting | bytes 192

commit v12 on v11

--- a/solution.py
+++ b/solution.py
@@ -268,10 +268,10 @@
 
     lax.fori_loop(0, 2, next_units, 0)
 
-    def last_units(step, _):
+    def far_units(step, _):
         @pl.when(step == 0)
         def _():
-            for k in range(5):
+            for k in range(4):
                 for copy in from_near(k, 1):
                     copy.wait_recv()
                 for copy in last_on[k]:
@@ -279,13 +279,27 @@
 
         @pl.when(step == 1)
         def _():
-            for copy in sum(last_on, []):
+            for copy in from_near(4, 1):
                 copy.wait_recv()
-
-        row_unit(37 + CHIPS * step, 27)
+            for copy in last_on[4]:
+                copy.start()
+            for copy in sum(last_on[:4], []):
+                copy.wait_recv()
+
+        row_unit(37 + CHIPS * step, 16)
         return 0
 
-    lax.fori_loop(0, 2, last_units, 0)
+    def rest_units(step, _):
+        @pl.when(step == 1)
+        def _():
+            for copy in last_on[4]:
+                copy.wait_recv()
+
+        row_unit(53 + CHIPS * step, len(REST))
+        return 0
+
+    lax.fori_loop(0, 2, far_units, 0)
+    lax.fori_loop(0, 2, rest_units, 0)
 
     def combined(values):
         top = jnp.max(values, axis=0)

time: 47.7 us -> 48 us (level)
  no operation moved by 1% of the time
where the time goes in v12:
time: 48 us; the launch traced here: 47.8 us
  Pallas kernels  46.1 us (96%)
  local copies, waits for them, and re-layouts  1.08 us (2%)
  between operations  0.64 us (1%)
    pallas_call x1, Pallas kernels, per_device(): pl.pallas_call(kernel, out_shape=(jax.ShapeDtypeStruct((1, ROWS), F32), j...  46.1 us
    unnamed x2, local copies, waits for them, and re-layouts  1.08 us

profile of v12, /device:TPU:1, one launch (start us, length us, event | category | flops | bytes accessed | tf_op | source)
XLA Modules:
  0.0 47.8 jit_solution(5147957195458834991)
XLA Ops:
  0.6 46.1 %shard_map.50 = (f32[1,256]{1,0:T(1,128)S(1)}, f32[1,24]{1,0:T(1,128)S(1)}) custom-call(bf16[256,256]{1,0:T(8,128)(2,1)} %gen_hbm.1, bf16[24,256]{1,0:T(8,128)(2,1)} %data_hbm.1, f32[1,24]{1,0:T(1,128)} %bitcast.5), custom_call_target="tpu_custom_call" | custom-call | tf_op jit(solution)/shard_map/pallas_call | solution.py:413
  46.8 0.6 %copy.7 = f32[256]{0:T(256)} copy(f32[256]{0:T(256)S(1)} %bitcast.3) | data formatting | bytes 2048
  47.3 0.5 %copy.8 = f32[24]{0:T(128)} copy(f32[24]{0:T(128)S(1)} %bitcast.4) | data formatting | bytes 192

commit v13 on v9

--- a/solution.py
+++ b/solution.py
@@ -30,9 +30,9 @@
 
 
 NEAR0 = [(0, 0), (0, 2), (0, -2), (2, 1), (2, -1), (-2, 1), (-2, -1), (0, 4)]
-FAR0 = [(4, 0), (2, 3), (2, -3), (-2, 3), (-2, -3)]
+FAR0 = [(4, 0), (2, 3), (2, -3), (-2, 3), (-2, -3), (4, 2), (4, -2)]
 NEAR2 = ([(0, 1), (2, 2), (-2, 2), (2, 0)], [(0, -1), (2, -2), (-2, -2), (-2, 0)])
-FAR2 = ([(0, 3), (4, 1), (2, 4)], [(0, -3), (4, -1), (-2, 4)])
+FAR2 = ([(0, 3), (4, 1), (4, 3), (2, 4)], [(0, -3), (4, -1), (4, -3), (-2, 4)])
 
 
 def shifted(offsets, dp, dq):
@@ -158,7 +158,7 @@
     def from_group(far):
         return [
             remote(
-                ref.at[pl.ds(0, (7, 5)[far])], ref.at[pl.ds(0, (7, 5)[far])],
+                ref.at[pl.ds(0, (7, 7)[far])], ref.at[pl.ds(0, (7, 7)[far])],
                 one_send.at[i, far], one_recv.at[i, far], sibling,
             )
             for i, ref in enumerate(refs)
@@ -174,9 +174,9 @@
         ]
 
     def send_near(i, far):
-        count = (8, 5)[far]
+        count = (8, 7)[far]
         for k in range(2):
-            to_near(k, far, count, 8 * far, (13, 37)[far] + k * count, near[1 - k])[i].start()
+            to_near(k, far, count, 8 * far, (15, 39)[far] + k * count, near[1 - k])[i].start()
         for side, ways in enumerate((NEAR2, FAR2)[far]):
             for dp, dq in ways:
                 held = slot_of(dp, dq + 2 * side - 1)
@@ -186,7 +186,7 @@
                 to_near(4, far, 1, slot_of(dp - hp, dq - hq), slot_of(dp, dq), in_plane(p - hp, q - hq))[i].start()
 
     def from_near(k, far):
-        return to_near(k, far, (8, 8, 4, 4, 0)[k] if not far else (5, 5, 3, 3, len(REST))[k], 0, 0, sibling)
+        return to_near(k, far, (8, 8, 4, 4, 0)[k] if not far else (7, 7, 4, 4, len(REST))[k], 0, 0, sibling)
 
     def to_sibling(k, start, count):
         return [
@@ -197,8 +197,8 @@
             for i, ref in enumerate(refs)
         ]
 
-    pieces = ((37, 5), (42, 5), (47, 3), (50, 3), (53, len(REST)))
-    passed_on = [to_sibling(0, 0, 8), to_sibling(1, 8, 5), to_sibling(2, 13, 24)]
+    pieces = ((39, 7), (46, 7), (53, 4), (57, 4), (61, len(REST)))
+    passed_on = [to_sibling(0, 0, 8), to_sibling(1, 8, 7), to_sibling(2, 15, 24)]
     last_on = [to_sibling(3 + k, *piece) for k, piece in enumerate(pieces)]
     for far in range(2):
         for i in range(2):
@@ -242,11 +242,11 @@
             for copy in passed_on[0] + passed_on[1]:
                 copy.wait_recv()
 
-        row_unit(CHIPS * step, 13, (0, 1, 3))
+        row_unit(CHIPS * step, 15, (0, 1, 3))
         return 0
 
     def first_opposite(step, _):
-        row_unit(CHIPS * step, 13, (2,))
+        row_unit(CHIPS * step, 15, (2,))
         return 0
 
     lax.fori_loop(0, 2, first_units, 0)
@@ -259,7 +259,7 @@
             for copy in passed_on[2]:
                 copy.wait_recv()
 
-        row_unit(13 + CHIPS * step, 24)
+        row_unit(15 + CHIPS * step, 24)
         return 0
 
     lax.fori_loop(0, 2, next_units, 0)
@@ -278,7 +278,7 @@
             for copy in sum(last_on, []):
                 copy.wait_recv()
 
-        row_unit(37 + CHIPS * step, 27)
+        row_unit(39 + CHIPS * step, 25)
         return 0
 
     lax.fori_loop(0, 2, last_units, 0)

time: 47.6 us -> 48.4 us (1.017)
  Pallas kernels: 45.8 us -> 46.6 us
    pallas_call x1, Pallas kernels: 45.8 us -> 46.6 us  [per_device(): pl.pallas_call(kernel, out_shape=(jax.ShapeDtypeStruct((1, ROWS), F32), j...]
where the time goes in v13:
time: 48.4 us; the launch traced here: 48.3 us
  Pallas kernels  46.6 us (96%)
  local copies, waits for them, and re-layouts  1.08 us (2%)
  between operations  0.64 us (1%)
    pallas_call x1, Pallas kernels, per_device(): pl.pallas_call(kernel, out_shape=(jax.ShapeDtypeStruct((1, ROWS), F32), j...  46.6 us
    unnamed x2, local copies, waits for them, and re-layouts  1.08 us

profile of v13, /device:TPU:1, one launch (start us, length us, event | category | flops | bytes accessed | tf_op | source)
XLA Modules:
  0.0 48.3 jit_solution(14124415553988499131)
XLA Ops:
  0.6 46.6 %shard_map.50 = (f32[1,256]{1,0:T(1,128)S(1)}, f32[1,24]{1,0:T(1,128)S(1)}) custom-call(bf16[256,256]{1,0:T(8,128)(2,1)} %gen_hbm.1, bf16[24,256]{1,0:T(8,128)(2,1)} %data_hbm.1, f32[1,24]{1,0:T(1,128)} %bitcast.5), custom_call_target="tpu_custom_call" | custom-call | tf_op jit(solution)/shard_map/pallas_call | solution.py:395
  47.2 0.6 %copy.7 = f32[256]{0:T(256)} copy(f32[256]{0:T(256)S(1)} %bitcast.3) | data formatting | bytes 2048
  47.8 0.5 %copy.8 = f32[24]{0:T(128)} copy(f32[24]{0:T(128)S(1)} %bitcast.4) | data formatting | bytes 192

commit v14 on v9

--- a/solution.py
+++ b/solution.py
@@ -340,7 +340,9 @@
 
     room = (batch_a, batch_b)
     batch_parts(BATCHES[0], room[0])
-    for i in range(8):
+    batch_send(0, room[0])
+    batch_parts(BATCHES[1], room[1])
+    for i in range(1, 8):
         if i < 7:
             batch_parts(BATCHES[i + 1], room[(i + 1) % 2])
         batch_send(i, room[i % 2])

time: 47.6 us -> 47.7 us (level)
  no operation moved by 1% of the time
where the time goes in v14:
time: 47.7 us; the launch traced here: 47.6 us
  Pallas kernels  45.9 us (96%)
  local copies, waits for them, and re-layouts  1.08 us (2%)
  between operations  0.64 us (1%)
    pallas_call x1, Pallas kernels, per_device(): pl.pallas_call(kernel, out_shape=(jax.ShapeDtypeStruct((1, ROWS), F32), j...  45.9 us
    unnamed x2, local copies, waits for them, and re-layouts  1.08 us

profile of v14, /device:TPU:1, one launch (start us, length us, event | category | flops | bytes accessed | tf_op | source)
XLA Modules:
  0.0 47.6 jit_solution(861101695637400795)
XLA Ops:
  0.6 45.9 %shard_map.50 = (f32[1,256]{1,0:T(1,128)S(1)}, f32[1,24]{1,0:T(1,128)S(1)}) custom-call(bf16[256,256]{1,0:T(8,128)(2,1)} %gen_hbm.1, bf16[24,256]{1,0:T(8,128)(2,1)} %data_hbm.1, f32[1,24]{1,0:T(1,128)} %bitcast.5), custom_call_target="tpu_custom_call" | custom-call | tf_op jit(solution)/shard_map/pallas_call | solution.py:397
  46.5 0.6 %copy.7 = f32[256]{0:T(256)} copy(f32[256]{0:T(256)S(1)} %bitcast.3) | data formatting | bytes 2048
  47.1 0.5 %copy.8 = f32[24]{0:T(128)} copy(f32[24]{0:T(128)S(1)} %bitcast.4) | data formatting | bytes 192
